TPU v7x, 128 devices: a whole 4x4x4 slice. The times are simulated.
128 devices in a mesh: dir: 8 (over z, y_lo), bl: 16 (over x, y_hi, core).
Axes of the slice: x: 4, y: 4 (y_hi: 2, y_lo: 2; y = y_hi * 2 + y_lo), z: 4, core: 2. Of those that a mesh axis runs over, the one named last changes fastest.
Arguments:
- observed: float32 [32, 2, 61440], P('dir', None, 'bl'), may hold values from -6 to 6
- baseline_uvw_rows: float32 [3, 131072], P(None, 'bl'), may hold values from -600 to 600
- frequencies: float32 [32], replicated, may hold values from 0.8 to 1.2
- source_offset: float32 [2, 256], replicated, may hold values from -0.05 to 0.05
- source_flux: float32 [32, 256], replicated, may hold values from 0.02 to 0.3
- source_group: int32 [256], replicated, may hold values from 0 to 7, as said below
- direction_gain: float32 [8, 32, 2, 512], P('dir'), may hold values from -4.2 to 4.2
- station_first: int32 [8192], replicated, may hold values from 0 to 511
- station_second: int32 [8192], replicated, may hold values from 0 to 511
- average_exponent: int32 [8192], replicated, may hold values from 0 to 4, as said below
- owner_plan: int32 [16, 16], replicated, may hold values from 0 to 15, as said below
Outputs:
- residual: float32 [32, 2, 61440], P('dir', None, 'bl')
Inputs may be any that keep to these rules, and one draw needn't show every extreme that they name: `source_group`: each of the 8 groups is named by exactly 32 sources. `average_exponent`: summed over the blocks that owner_plan gives one owner, the averaged rows are at most 3840, and some owner has exactly 3840. Each row of owner_plan names every owner exactly once.
All inputs are finite; a program needn't handle non-finite values.
Results may differ from a plain program's by a relative error of at most 0.0003.
Values sent between devices are 32-bit elements; how exact they have to be, the bound alone decides.
No kernel may reach another device: no remote copies, remote signals or barrier semaphores. Data moves between devices by JAX's collectives and lax.ppermute only.
A program may use at most 64 MiB of HBM per device.

v0:
```python
import jax
import jax.numpy as jnp
from jax import lax
from jax.sharding import Mesh
from jax.sharding import PartitionSpec as P

TIME_SAMPLES = 16
SRC_GRP = 32
BL_DEV = 512
BL = ("bl_0", "bl_1", "bl_2")


def in_blocks(shard, dim, devices):
    shape = shard.shape
    tiles = shard.reshape(*shape[:dim], devices, shape[dim] // devices, *shape[dim + 1 :])
    return jnp.moveaxis(tiles, dim, 0)


def sum_at_owner(shard, axis, dim):
    devices = lax.axis_size(axis)
    tiles = lax.all_to_all(in_blocks(shard, dim, devices), axis, 0, 0, tiled=True)
    return jnp.sum(tiles, axis=0)


def in_order(tiles, dim):
    shape = list(tiles.shape[1:])
    shape[dim] *= tiles.shape[0]
    return jnp.moveaxis(tiles, 0, dim).reshape(shape)


def exchange_in_order(tiles, axes, order):
    inside = tiles.shape[1:]
    out = tiles.reshape(*(lax.axis_size(a) for a in axes), *inside)
    for k in order:
        out = lax.all_to_all(out, axes[k], k, k, tiled=True)
    return out.reshape(-1, *inside)


def exchange_by_chip(shard, groups, order, split_dim, concat_dim):
    devices = lax.axis_size(groups[0]) * lax.axis_size(groups[1])
    tiles = in_blocks(shard, split_dim, devices)
    return in_order(exchange_in_order(tiles, groups, order), concat_dim)


def layout_tables(average_exponent, owner_plan, owners_total, block_len):
    factor = jnp.left_shift(jnp.ones_like(average_exponent), average_exponent)
    row_count = TIME_SAMPLES // factor
    grouped = row_count.reshape(owners_total, owners_total, block_len)
    block_rows = jnp.sum(grouped, axis=2, dtype=jnp.int32)
    in_block = (jnp.cumsum(grouped, axis=2, dtype=jnp.int32) - grouped).reshape(-1)
    owner_ids = jnp.arange(owners_total, dtype=jnp.int32)
    matches = (owner_plan[:, :, None] == owner_ids[None, None, :]).astype(jnp.int32)
    to_owner = jnp.sum(block_rows[:, :, None] * matches, axis=1, dtype=jnp.int32)
    before = jnp.cumsum(to_owner, axis=0, dtype=jnp.int32) - to_owner
    return (in_block, before, matches)


def compact_matrix(exponent, start_in, block_count, slot_rows):
    shaped_exp = exponent.reshape(block_count, -1)
    shaped_start = start_in.reshape(block_count, -1)
    sample_index = jnp.arange(TIME_SAMPLES, dtype=jnp.int32)
    target = (
        shaped_start[:, :, None]
        + jnp.right_shift(sample_index[None, None, :], shaped_exp[:, :, None])
    ).reshape(block_count, slot_rows)
    divisor = jnp.left_shift(jnp.ones_like(shaped_exp), shaped_exp).astype(jnp.float32)
    weight = jnp.broadcast_to(
        (1.0 / divisor)[:, :, None], (block_count, shaped_exp.shape[1], TIME_SAMPLES)
    ).reshape(block_count, slot_rows)
    slots = jnp.arange(slot_rows, dtype=jnp.int32)
    return (target[:, :, None] == slots[None, None, :]).astype(jnp.float32) * weight[:, :, None]


def compact_rows(model_rows, matrix):
    leading = model_rows.shape[0]
    block_count = matrix.shape[0]
    shaped = model_rows.reshape(leading, 2, block_count, matrix.shape[1])
    return jnp.einsum("czkr,krs->czks", shaped, matrix, precision=lax.Precision.HIGHEST)


def pack_pieces(arrived, starts, capacity):
    leading = arrived.shape[0]
    piece_count = arrived.shape[2]
    slot_rows = arrived.shape[3]
    buffer = jnp.zeros((leading, 2, capacity + slot_rows), jnp.float32)

    def place_piece(index, current):
        piece = lax.dynamic_index_in_dim(arrived, index, 2, keepdims=False)
        return lax.dynamic_update_slice_in_dim(current, piece, starts[index], 2)

    buffer = lax.fori_loop(0, piece_count, place_piece, buffer)
    return buffer[:, :, :capacity]


def station_picker(ids, station_total):
    stations = jnp.arange(station_total, dtype=jnp.int32)
    return (stations[:, None] == ids[None, :]).astype(jnp.float32)


def select_sources(source_offset, source_flux, source_group, group_index):
    chosen = (source_group == group_index).astype(jnp.int32)
    position = jnp.cumsum(chosen, dtype=jnp.int32) - 1
    picker = (
        (position[None, :] == jnp.arange(SRC_GRP, dtype=jnp.int32)[:, None]) & (chosen[None, :] > 0)
    ).astype(jnp.float32)
    chosen_offset = jnp.dot(source_offset, picker.T, precision=lax.Precision.HIGHEST)
    chosen_flux = jnp.dot(source_flux, picker.T, precision=lax.Precision.HIGHEST)
    return (chosen_offset, chosen_flux)


def predict_rows(coords, offsets, flux, frequencies, gains, first_pick, second_pick, span_rows):
    east_offset = offsets[0]
    north_offset = offsets[1]
    depth_term = jnp.sqrt(1.0 - east_offset * east_offset - north_offset * north_offset) - 1.0
    total_rows = coords.shape[1]
    row_block = min(total_rows, 1024)

    def row_piece(coord_block):
        phase_base = (
            2.0
            * jnp.pi
            * (
                east_offset[:, None] * coord_block[0][None, :]
                + north_offset[:, None] * coord_block[1][None, :]
                + depth_term[:, None] * coord_block[2][None, :]
            )
        )
        angles = frequencies[:, None, None] * phase_base[None, :, :]
        real_sum = jnp.einsum("ck,ckr->cr", flux, jnp.cos(angles), precision=lax.Precision.HIGHEST)
        imag_sum = -jnp.einsum("ck,ckr->cr", flux, jnp.sin(angles), precision=lax.Precision.HIGHEST)
        return (real_sum, imag_sum)

    blocks = jnp.transpose(coords.reshape(3, -1, row_block), (1, 0, 2))
    real_all, imag_all = lax.map(row_piece, blocks)
    real_all = jnp.transpose(real_all, (1, 0, 2)).reshape(span_rows, total_rows)
    imag_all = jnp.transpose(imag_all, (1, 0, 2)).reshape(span_rows, total_rows)
    gain_first = jnp.einsum("czs,sb->czb", gains, first_pick, precision=lax.Precision.HIGHEST)
    gain_second = jnp.einsum("czs,sb->czb", gains, second_pick, precision=lax.Precision.HIGHEST)
    gain_real = gain_first[:, 0] * gain_second[:, 0] + gain_first[:, 1] * gain_second[:, 1]
    gain_imag = gain_first[:, 1] * gain_second[:, 0] - gain_first[:, 0] * gain_second[:, 1]
    gain_real = jnp.repeat(gain_real, TIME_SAMPLES, axis=1)
    gain_imag = jnp.repeat(gain_imag, TIME_SAMPLES, axis=1)
    out_real = real_all * gain_real - imag_all * gain_imag
    out_imag = real_all * gain_imag + imag_all * gain_real
    return jnp.stack([out_real, out_imag], axis=1)


def on_device(
    observed,
    baseline_uvw_rows,
    frequencies,
    source_offset,
    source_flux,
    source_group,
    direction_gain,
    station_first,
    station_second,
    average_exponent,
    owner_plan,
):
    owners_total = lax.axis_size(BL)
    owner_index = lax.axis_index(BL)
    block_len = BL_DEV // owners_total
    slot_rows = block_len * TIME_SAMPLES
    capacity = observed.shape[2]
    local_channels = observed.shape[0]
    station_total = direction_gain.shape[3]
    in_block, before, matches = layout_tables(average_exponent, owner_plan, owners_total, block_len)
    chosen_offset, chosen_flux = select_sources(
        source_offset, source_flux, source_group, lax.axis_index("dir")
    )
    gains = direction_gain[0]
    owner_ids = jnp.arange(owners_total, dtype=jnp.int32)
    held_starts = before[:, owner_index]
    own_begin = owner_index * BL_DEV
    own_first = lax.dynamic_slice_in_dim(station_first, own_begin, BL_DEV, 0)
    own_second = lax.dynamic_slice_in_dim(station_second, own_begin, BL_DEV, 0)
    own_exponent = lax.dynamic_slice_in_dim(average_exponent, own_begin, BL_DEV, 0)
    own_in_block = lax.dynamic_slice_in_dim(in_block, own_begin, BL_DEV, 0)
    destination = owner_plan[owner_index]
    first_pick = station_picker(own_first, station_total)
    second_pick = station_picker(own_second, station_total)
    channel_sum = sum_at_owner(
        predict_rows(
            baseline_uvw_rows,
            chosen_offset,
            chosen_flux,
            frequencies,
            gains,
            first_pick,
            second_pick,
            local_channels * lax.axis_size("dir"),
        ),
        "dir",
        0,
    )
    matrix = compact_matrix(own_exponent, own_in_block, owners_total, slot_rows)
    compacted = compact_rows(channel_sum, matrix)
    routing = (destination[:, None] == owner_ids[None, :]).astype(jnp.float32)
    arrived = exchange_by_chip(
        jnp.einsum("czks,ko->czos", compacted, routing, precision=lax.Precision.HIGHEST),
        (("bl_0", "bl_1"), "bl_2"),
        (1, 0),
        2,
        2,
    )
    summed = pack_pieces(arrived, held_starts, capacity)
    return observed - summed


def solution(mesh):
    torus = Mesh(mesh.devices.reshape(mesh.shape["dir"], 4, 2, 2), ("dir", "bl_0", "bl_1", "bl_2"))
    in_specs = (
        P("dir", None, BL),
        P(None, BL),
        P(),
        P(),
        P(),
        P(),
        P("dir", None, None, None),
        P(),
        P(),
        P(),
        P(),
    )
    out_specs = P("dir", None, BL)
    return jax.shard_map(
        on_device, mesh=torus, in_specs=in_specs, out_specs=out_specs, check_vma=False
    )
```

profile of v0, /device:TPU:1, one launch (start us, length us, event | category | flops | bytes accessed | tf_op | source)
XLA Modules:
  0.0 451.8 jit_solution(5840937714466675160)
XLA Ops:
  2.6 4.6 %broadcast_in_dim.24 = f32[32,512,16]{2,1,0:T(8,128)} broadcast(f32[32,512]{1,0:T(8,128)S(1)} %get-tuple-element.213), dimensions={0,1} | broadcast | bytes 1114112 | tf_op jit(solution)/shard_map/broadcast_in_dim | solution.py:142
  7.1 6.6 %reshape.305 = f32[8,4,1,8192]{3,1,0,2:T(4,128)S(1)} reshape(f32[32,512,16]{2,1,0:T(8,128)} %broadcast_in_dim.24) | data formatting | bytes 2097152 | tf_op jit(solution)/shard_map/reshape | solution.py:142
  13.7 4.6 %broadcast_in_dim.23 = f32[32,512,16]{2,1,0:T(8,128)} broadcast(f32[32,512]{1,0:T(8,128)S(1)} %get-tuple-element.214), dimensions={0,1} | broadcast | bytes 1114112 | tf_op jit(solution)/shard_map/broadcast_in_dim | solution.py:141
  18.3 6.6 %reshape.303 = f32[8,4,1,8192]{3,1,0,2:T(4,128)S(1)} reshape(f32[32,512,16]{2,1,0:T(8,128)} %broadcast_in_dim.23) | data formatting | bytes 2097152 | tf_op jit(solution)/shard_map/reshape | solution.py:141
  26.0 290.3 %while.25 = (s32[]{:T(128)}, f32[8,32,1024]{2,1,0:T(8,128)}, f32[8,32,1024]{2,1,0:T(8,128)}, f32[32]{0:T(128)S(1)}, f32[1,32]{1,0:T(1,128)S(1)}, /*index=5*/f32[...) while((s32[]{:T(128)}, f32[8,32,1024]{2,1,0:T(8,128)}, ...), condition=%wide.region_4.5_spmd, body=%wide.region_3.4_spmd.sunk | while | flops 27492356 | bytes 1226017 | solution.py:134
  26.9 17.3 %fusion.52 = f32[32,1,1024]{2,1,0:T(1,128)S(1)} fusion(f32[32,32,1]{1,2,0:T(1,128)S(1)} %bitcast.137, f32[32,1024]{1,0:T(8,128)S(1)} %add_multiply_fusion.2, f32[32]{0:T(128)S(1)} %get-tuple-element.341), kind=kOutput, calls=%fused_computation.3.clone.1 | convolution fusion | flops 13631488 | bytes 266368 | tf_op jit(solution)/shard_map/while/body/eval_jaxpr/ck,ckr->cr/dot_general | solution.py:130
  44.3 17.2 %fusion.53 = f32[32,1,1024]{2,1,0:T(1,128)S(1)} fusion(f32[32,32,1]{1,2,0:T(1,128)S(1)} %bitcast.138, f32[32,1024]{1,0:T(8,128)S(1)} %add_multiply_fusion.2, f32[32]{0:T(128)S(1)} %get-tuple-element.341), kind=kOutput, calls=%fused_computation.2.clone.1 | convolution fusion | flops 13631488 | bytes 266368 | tf_op jit(solution)/shard_map/while/body/eval_jaxpr/ck,ckr->cr/dot_general | solution.py:129
  63.2 17.3 %fusion.52 = f32[32,1,1024]{2,1,0:T(1,128)S(1)} fusion(f32[32,32,1]{1,2,0:T(1,128)S(1)} %bitcast.137, f32[32,1024]{1,0:T(8,128)S(1)} %add_multiply_fusion.2, f32[32]{0:T(128)S(1)} %get-tuple-element.341), kind=kOutput, calls=%fused_computation.3.clone.1 | convolution fusion | flops 13631488 | bytes 266368 | tf_op jit(solution)/shard_map/while/body/eval_jaxpr/ck,ckr->cr/dot_general | solution.py:130
  80.6 17.2 %fusion.53 = f32[32,1,1024]{2,1,0:T(1,128)S(1)} fusion(f32[32,32,1]{1,2,0:T(1,128)S(1)} %bitcast.138, f32[32,1024]{1,0:T(8,128)S(1)} %add_multiply_fusion.2, f32[32]{0:T(128)S(1)} %get-tuple-element.341), kind=kOutput, calls=%fused_computation.2.clone.1 | convolution fusion | flops 13631488 | bytes 266368 | tf_op jit(solution)/shard_map/while/body/eval_jaxpr/ck,ckr->cr/dot_general | solution.py:129
  99.5 17.3 %fusion.52 = f32[32,1,1024]{2,1,0:T(1,128)S(1)} fusion(f32[32,32,1]{1,2,0:T(1,128)S(1)} %bitcast.137, f32[32,1024]{1,0:T(8,128)S(1)} %add_multiply_fusion.2, f32[32]{0:T(128)S(1)} %get-tuple-element.341), kind=kOutput, calls=%fused_computation.3.clone.1 | convolution fusion | flops 13631488 | bytes 266368 | tf_op jit(solution)/shard_map/while/body/eval_jaxpr/ck,ckr->cr/dot_general | solution.py:130
  116.9 17.2 %fusion.53 = f32[32,1,1024]{2,1,0:T(1,128)S(1)} fusion(f32[32,32,1]{1,2,0:T(1,128)S(1)} %bitcast.138, f32[32,1024]{1,0:T(8,128)S(1)} %add_multiply_fusion.2, f32[32]{0:T(128)S(1)} %get-tuple-element.341), kind=kOutput, calls=%fused_computation.2.clone.1 | convolution fusion | flops 13631488 | bytes 266368 | tf_op jit(solution)/shard_map/while/body/eval_jaxpr/ck,ckr->cr/dot_general | solution.py:129
  135.8 17.3 %fusion.52 = f32[32,1,1024]{2,1,0:T(1,128)S(1)} fusion(f32[32,32,1]{1,2,0:T(1,128)S(1)} %bitcast.137, f32[32,1024]{1,0:T(8,128)S(1)} %add_multiply_fusion.2, f32[32]{0:T(128)S(1)} %get-tuple-element.341), kind=kOutput, calls=%fused_computation.3.clone.1 | convolution fusion | flops 13631488 | bytes 266368 | tf_op jit(solution)/shard_map/while/body/eval_jaxpr/ck,ckr->cr/dot_general | solution.py:130
  153.1 17.2 %fusion.53 = f32[32,1,1024]{2,1,0:T(1,128)S(1)} fusion(f32[32,32,1]{1,2,0:T(1,128)S(1)} %bitcast.138, f32[32,1024]{1,0:T(8,128)S(1)} %add_multiply_fusion.2, f32[32]{0:T(128)S(1)} %get-tuple-element.341), kind=kOutput, calls=%fused_computation.2.clone.1 | convolution fusion | flops 13631488 | bytes 266368 | tf_op jit(solution)/shard_map/while/body/eval_jaxpr/ck,ckr->cr/dot_general | solution.py:129
  172.0 17.3 %fusion.52 = f32[32,1,1024]{2,1,0:T(1,128)S(1)} fusion(f32[32,32,1]{1,2,0:T(1,128)S(1)} %bitcast.137, f32[32,1024]{1,0:T(8,128)S(1)} %add_multiply_fusion.2, f32[32]{0:T(128)S(1)} %get-tuple-element.341), kind=kOutput, calls=%fused_computation.3.clone.1 | convolution fusion | flops 13631488 | bytes 266368 | tf_op jit(solution)/shard_map/while/body/eval_jaxpr/ck,ckr->cr/dot_general | solution.py:130
  189.4 17.2 %fusion.53 = f32[32,1,1024]{2,1,0:T(1,128)S(1)} fusion(f32[32,32,1]{1,2,0:T(1,128)S(1)} %bitcast.138, f32[32,1024]{1,0:T(8,128)S(1)} %add_multiply_fusion.2, f32[32]{0:T(128)S(1)} %get-tuple-element.341), kind=kOutput, calls=%fused_computation.2.clone.1 | convolution fusion | flops 13631488 | bytes 266368 | tf_op jit(solution)/shard_map/while/body/eval_jaxpr/ck,ckr->cr/dot_general | solution.py:129
  208.3 17.3 %fusion.52 = f32[32,1,1024]{2,1,0:T(1,128)S(1)} fusion(f32[32,32,1]{1,2,0:T(1,128)S(1)} %bitcast.137, f32[32,1024]{1,0:T(8,128)S(1)} %add_multiply_fusion.2, f32[32]{0:T(128)S(1)} %get-tuple-element.341), kind=kOutput, calls=%fused_computation.3.clone.1 | convolution fusion | flops 13631488 | bytes 266368 | tf_op jit(solution)/shard_map/while/body/eval_jaxpr/ck,ckr->cr/dot_general | solution.py:130
  225.7 17.2 %fusion.53 = f32[32,1,1024]{2,1,0:T(1,128)S(1)} fusion(f32[32,32,1]{1,2,0:T(1,128)S(1)} %bitcast.138, f32[32,1024]{1,0:T(8,128)S(1)} %add_multiply_fusion.2, f32[32]{0:T(128)S(1)} %get-tuple-element.341), kind=kOutput, calls=%fused_computation.2.clone.1 | convolution fusion | flops 13631488 | bytes 266368 | tf_op jit(solution)/shard_map/while/body/eval_jaxpr/ck,ckr->cr/dot_general | solution.py:129
  244.6 17.3 %fusion.52 = f32[32,1,1024]{2,1,0:T(1,128)S(1)} fusion(f32[32,32,1]{1,2,0:T(1,128)S(1)} %bitcast.137, f32[32,1024]{1,0:T(8,128)S(1)} %add_multiply_fusion.2, f32[32]{0:T(128)S(1)} %get-tuple-element.341), kind=kOutput, calls=%fused_computation.3.clone.1 | convolution fusion | flops 13631488 | bytes 266368 | tf_op jit(solution)/shard_map/while/body/eval_jaxpr/ck,ckr->cr/dot_general | solution.py:130
  262.0 17.2 %fusion.53 = f32[32,1,1024]{2,1,0:T(1,128)S(1)} fusion(f32[32,32,1]{1,2,0:T(1,128)S(1)} %bitcast.138, f32[32,1024]{1,0:T(8,128)S(1)} %add_multiply_fusion.2, f32[32]{0:T(128)S(1)} %get-tuple-element.341), kind=kOutput, calls=%fused_computation.2.clone.1 | convolution fusion | flops 13631488 | bytes 266368 | tf_op jit(solution)/shard_map/while/body/eval_jaxpr/ck,ckr->cr/dot_general | solution.py:129
  280.9 17.3 %fusion.52 = f32[32,1,1024]{2,1,0:T(1,128)S(1)} fusion(f32[32,32,1]{1,2,0:T(1,128)S(1)} %bitcast.137, f32[32,1024]{1,0:T(8,128)S(1)} %add_multiply_fusion.2, f32[32]{0:T(128)S(1)} %get-tuple-element.341), kind=kOutput, calls=%fused_computation.3.clone.1 | convolution fusion | flops 13631488 | bytes 266368 | tf_op jit(solution)/shard_map/while/body/eval_jaxpr/ck,ckr->cr/dot_general | solution.py:130
  298.3 17.2 %fusion.53 = f32[32,1,1024]{2,1,0:T(1,128)S(1)} fusion(f32[32,32,1]{1,2,0:T(1,128)S(1)} %bitcast.138, f32[32,1024]{1,0:T(8,128)S(1)} %add_multiply_fusion.2, f32[32]{0:T(128)S(1)} %get-tuple-element.341), kind=kOutput, calls=%fused_computation.2.clone.1 | convolution fusion | flops 13631488 | bytes 266368 | tf_op jit(solution)/shard_map/while/body/eval_jaxpr/ck,ckr->cr/dot_general | solution.py:129
  316.2 1.8 copy.49
  319.8 1.8 copy.46
  323.4 1.8 multiply_subtract_fusion
  327.2 7.0 %all-to-all-start = ((f32[8,4,2,8192]{3,1,2,0:T(4,128)}), f32[8,4,2,8192]{3,1,2,0:T(4,128)S(1)}, u32[]{:S(2)}, u32[]{:S(2)}) async-start(f32[8,4,2,8192]{3,1,2,0:T(4,128)} %copy.50), calls=%async_computation | async-start | bytes 4194304 | tf_op jit(solution)/shard_map/all_to_all | solution.py:21
  334.8 3.0 reduce_window_sum.41
  339.1 21.2 %all-to-all-done = f32[8,4,2,8192]{3,1,2,0:T(4,128)S(1)} async-done(((f32[8,4,2,8192]{3,1,2,0:T(4,128)}), f32[8,4,2,8192]{3,1,2,0:T(4,128)S(1)}, u32[]{:S(2)}, u32[]{:S(2)}) %all-to-all-start) | async-done | bytes 2097184 | tf_op jit(solution)/shard_map/all_to_all | solution.py:21
  360.8 11.5 %fusion.12 = f32[4,2,16,512]{3,0,1,2:T(4,128)S(1)} fusion(f32[16,512]{1,0:T(8,128)S(1)} %mul.179, s32[16,512]{1,0:T(8,128)S(1)} %shift-right-arithmetic_add_fusion, f32[2,1,16,4,512]{4,3,2,1,0:T(4,128)S(1)} %bitcast.133), kind=kOutput, calls=%fused_computation.25 | convolution fusion | flops 411041792 | bytes 589824 | tf_op jit(solution)/shard_map/czkr,krs->czks/dot_general | solution.py:78
  372.9 5.4 %all_to_all.15 = f32[8,2,4,2,1,512]{5,0,3,2,4,1:T(8,128)S(1)} all-to-all(f32[8,2,4,2,1,512]{5,0,3,2,4,1:T(8,128)S(1)} %copy.54), channel_id=1, replica_groups=mesh['dir'=8,'bl_0'=4,'bl_1'=2,'bl_2'=2] {'bl_2'}, dimensions={1} | all-to-all | bytes 524288 | tf_op jit(solution)/shard_map/all_to_all | solution.py:35
  379.2 6.4 %all-to-all-start.2 = ((f32[8,2,4,2,1,512]{5,1,3,2,4,0:T(2,128)}), f32[8,2,4,2,1,512]{5,1,3,2,4,0:T(2,128)S(1)}, u32[]{:S(2)}, u32[]{:S(2)}) async-start(f32[8,2,4,2,1,512]{5,1,3,2,4,0:T(2,128)} %copy.55), calls=%async_computation.2 | async-start | bytes 524288 | tf_op jit(solution)/shard_map/all_to_all | solution.py:35
  386.3 6.7 %all-to-all-done.2 = f32[8,2,4,2,1,512]{5,1,3,2,4,0:T(2,128)S(1)} async-done(((f32[8,2,4,2,1,512]{5,1,3,2,4,0:T(2,128)}), f32[8,2,4,2,1,512]{5,1,3,2,4,0:T(2,128)S(1)}, u32[]{:S(2)}, u32[]{:S(2)}) %all-to-all-start.2) | async-done | bytes 262176 | tf_op jit(solution)/shard_map/all_to_all | solution.py:35
  393.2 57.8 %while.26 = (s32[]{:T(128)}, f32[4,2,4352]{2,1,0:T(2,128)S(1)}, f32[4,2,16,512]{3,1,0,2:T(2,128)S(1)}, s32[16]{0:T(128)S(1)}, s32[]{:T(128)}, /*index=5*/s32[]{:T(128)}, s32[]{:T(128)}) while((s32[]{:T(128)}, f32[4,2,4352]{2,1,0:T(2,128)S(1)}, f32[4,2,16,512]{3,1,0,2:T(2,128)S(1)}, s32[16]{0:T(128)S(1)}, s32[]{:T(128)}, ...), condition=%wide.region_10.11_spmd, body=%wide.region_9.10_spmd.sunk | while | flops 5 | bytes 65667 | solution.py:91
  (139 shorter events, 52.1 us)
Async XLA Ops:
  0.0 1.6 copy-start
  18.3 6.7 %copy-start.5 = (s32[256]{0:T(256)S(1)}, s32[256]{0:T(256)}, u32[]{:S(2)}) copy-start(s32[256]{0:T(256)} %param.20) | copy-start | bytes 3076
  18.3 7.3 %copy-start.6 = (f32[2,256]{1,0:T(2,128)S(1)}, f32[2,256]{1,0:T(2,128)}, u32[]{:S(2)}) copy-start(f32[2,256]{1,0:T(2,128)} %param.18) | copy-start | bytes 6148
  18.3 7.5 %copy-start.3 = (f32[32,256]{1,0:T(8,128)S(1)}, f32[32,256]{1,0:T(8,128)}, u32[]{:S(2)}) copy-start(f32[32,256]{1,0:T(8,128)} %param.19) | copy-start | bytes 98308
  18.3 7.7 %copy-start.7 = (f32[32]{0:T(128)S(1)}, f32[32]{0:T(128)}, u32[]{:S(2)}) copy-start(f32[32]{0:T(128)} %param.17) | copy-start | bytes 388
  325.7 8.6 %copy-start.2 = (s32[8192]{0:T(1024)S(1)}, s32[8192]{0:T(1024)}, u32[]{:S(2)}) copy-start(s32[8192]{0:T(1024)} %param.24) | copy-start | bytes 98308
  327.2 11.9 %copy-start.4 = (s32[16,16]{1,0:T(8,128)S(1)}, s32[16,16]{1,0:T(8,128)}, u32[]{:S(2)}) copy-start(s32[16,16]{1,0:T(8,128)} %param.25) | copy-start | bytes 3076
  327.2 33.1 %all-to-all-start = ((f32[8,4,2,8192]{3,1,2,0:T(4,128)}), f32[8,4,2,8192]{3,1,2,0:T(4,128)S(1)}, u32[]{:S(2)}, u32[]{:S(2)}) async-start(f32[8,4,2,8192]{3,1,2,0:T(4,128)} %copy.50), calls=%async_computation | async-start | bytes 4194304 | tf_op jit(solution)/shard_map/all_to_all | solution.py:21
  372.2 78.8 %copy-start.1 = (f32[4,2,3840]{2,1,0:T(2,128)S(1)}, f32[4,2,3840]{2,1,0:T(2,128)}, u32[]{:S(2)}) copy-start(f32[4,2,3840]{2,1,0:T(2,128)} %param.15) | copy-start | bytes 368644
  379.2 13.8 %all-to-all-start.2 = ((f32[8,2,4,2,1,512]{5,1,3,2,4,0:T(2,128)}), f32[8,2,4,2,1,512]{5,1,3,2,4,0:T(2,128)S(1)}, u32[]{:S(2)}, u32[]{:S(2)}) async-start(f32[8,2,4,2,1,512]{5,1,3,2,4,0:T(2,128)} %copy.55), calls=%async_computation.2 | async-start | bytes 524288 | tf_op jit(solution)/shard_map/all_to_all | solution.py:35
where the time goes:
time: 453 us; the launch traced here: 452 us
  matrix products  290 us (64%)
  local copies, waits for them, and re-layouts  66.4 us (15%)
  loops' own time  33.9 us (7%)
  waiting for transfers between devices  27.9 us (6%)
  other arithmetic  14.9 us (3%)
  starting transfers between devices  13.4 us (3%)
  blocking collectives  5.45 us (1%)
    dot_general x8, matrix products, row_piece(): jnp.einsum('ck,ckr->cr', flux, jnp.sin(angles), precision=lax.Precision.H...  139 us
    dot_general x8, matrix products, row_piece(): jnp.einsum('ck,ckr->cr', flux, jnp.cos(angles), precision=lax.Precision.H...  138 us
    another operation x1, loops' own time, pack_pieces(): buffer = lax.fori_loop(0, piece_count, place_piece, buffer)  33.7 us
    all_to_all x1, waiting for transfers between devices, sum_at_owner(): lax.all_to_all(in_blocks(shard, dim, devices), axis, 0, 0, tiled=True)  21.2 us
    dynamic_update_slice x16, local copies, waits for them, and re-layouts, place_piece(): return lax.dynamic_update_slice_in_dim(current, piece, starts[index], 2)  13.3 us
    dot_general x1, matrix products, compact_rows(): jnp.einsum('czkr,krs->czks', shaped, matrix, precision=lax.Precision.HIGH...  11.5 us
    dynamic_slice x16, local copies, waits for them, and re-layouts, place_piece(): return lax.dynamic_update_slice_in_dim(current, piece, starts[index], 2)  10.7 us
  transfers between devices with their start and end apart: 2, of which 2 were waited for; matrix products, arithmetic and copies ran while one was open for 1% of the time, Pallas kernels for 0%

commit v1 on v0

v1 whole, which is shorter than its diff:
```python
import functools

import jax
import jax.numpy as jnp
from jax import lax
from jax.experimental import pallas as pl
from jax.experimental.pallas import tpu as pltpu
from jax.sharding import PartitionSpec as P


TIME = 16
GROUPS = 8
PER_GROUP = 32
CHANNELS = 4
BLOCK_BASELINES = 32
SUB = 16
WINDOW = 384

POLE = 0.2500051432960012
LINE0 = 0.9326632751760481
LINE1 = 0.23550642249107842
SCALE = 2.4653076166502004

VMEM = pl.BlockSpec(memory_space=pltpu.VMEM)
SMEM = pl.BlockSpec(memory_space=pltpu.SMEM)


def split3(values):
    high = values.astype(jnp.bfloat16)
    rest = values - high.astype(jnp.float32)
    middle = rest.astype(jnp.bfloat16)
    low = (rest - middle.astype(jnp.float32)).astype(jnp.bfloat16)
    return high, middle, low


def route_kernel(plan_ref, uvw_ref, out_ref):
    owners = out_ref.shape[0]
    rows = out_ref.shape[2]
    for k in range(owners):
        out_ref[plan_ref[k]] = uvw_ref[:, k * rows : (k + 1) * rows]


def main_kernel(
    offset_ref,
    flux_ref,
    freq_ref,
    total_ref,
    base_ref,
    uvw_ref,
    gain_ref,
    table_ref,
    observed_ref,
    out_ref,
    u_ref,
    wide_ref,
    x_ref,
    model_ref,
    slot_ref,
):
    sources = uvw_ref.shape[0]
    baselines = gain_ref.shape[2]
    stations = gain_ref.shape[2]
    gc = gain_ref.shape[0]
    rows_of = 2 * gc + 16
    lanes = SUB * TIME
    tiles = baselines // (8 * SUB)
    halves = lanes // 128

    for p in range(sources):
        for half in range(2):
            sub = 2 * p + half
            q, s = sub // 8, sub % 8
            for d in range(3):
                u_ref[d, s : s + 1, q * lanes : (q + 1) * lanes] = uvw_ref[
                    p, d : d + 1, half * lanes : (half + 1) * lanes
                ]

    gain_rows = jnp.concatenate([gain_ref[:, 0, :], gain_ref[:, 1, :]], axis=0)
    pieces = jnp.concatenate(split3(gain_rows), axis=0)
    station = lax.broadcasted_iota(jnp.int32, (stations, baselines), 0)

    def picked(row):
        ids = table_ref[row : row + 1, :]
        one_hot = (station == ids).astype(jnp.float32).astype(jnp.bfloat16)
        found = jnp.dot(pieces, one_hot, preferred_element_type=jnp.float32)
        n = 2 * gc
        return found[:n] + found[n : 2 * n] + found[2 * n :]

    first = picked(0)
    second = picked(1)
    pair_real = first[:gc] * second[:gc] + first[gc:] * second[gc:]
    pair_imag = first[gc:] * second[:gc] - first[:gc] * second[gc:]
    starts = table_ref[2:3, :].astype(jnp.float32)
    inverse = table_ref[3:4, :].astype(jnp.float32) * (1.0 / TIME)
    narrow = jnp.concatenate(
        [pair_real, pair_imag, starts, inverse, jnp.zeros((14, baselines), jnp.float32)], axis=0
    )
    narrow = jnp.concatenate(split3(narrow), axis=0)
    per_tile = 8 * SUB
    width = per_tile * TIME
    spread = (
        lax.broadcasted_iota(jnp.int32, (per_tile, width), 0)
        == lax.broadcasted_iota(jnp.int32, (per_tile, width), 1) // TIME
    ).astype(jnp.float32).astype(jnp.bfloat16)
    for q in range(tiles):
        wide = jnp.dot(
            narrow[:, q * per_tile : (q + 1) * per_tile], spread, preferred_element_type=jnp.float32
        )
        wide = wide[:rows_of] + wide[rows_of : 2 * rows_of] + wide[2 * rows_of :]
        for s in range(8):
            for h in range(halves):
                left = s * lanes + h * 128
                wide_ref[h, pl.ds(q * 8 + s, rows_of, stride=8 * tiles), :] = wide[
                    :, left : left + 128
                ]

    model_ref[...] = jnp.zeros_like(model_ref)

    def group(g, carry):
        for k in range(PER_GROUP):
            i = g * PER_GROUP + k
            x_ref[k] = (
                u_ref[0] * offset_ref[0, i]
                + u_ref[1] * offset_ref[1, i]
                + u_ref[2] * offset_ref[2, i]
            )

        def channel(c, carry):
            freq = freq_ref[c]
            a = jnp.zeros((8, tiles * lanes), jnp.float32)
            b = jnp.zeros((8, tiles * lanes), jnp.float32)
            for k in range(PER_GROUP):
                y = x_ref[k] * freq
                t = y - jnp.round(y)
                q = t * t
                tangent = t * (pltpu.reciprocal(POLE - q, approx=True) + (LINE1 * q + LINE0))
                w = flux_ref[c, g * PER_GROUP + k] * pltpu.reciprocal(
                    tangent * tangent + SCALE, approx=True
                )
                a = a + w
                b = b + w * tangent
            cos_sum = (2.0 * SCALE) * a - total_ref[c, g]
            sin_sum = (2.0 * SCALE**0.5) * b
            real_row = (g * CHANNELS + c) * 8 * tiles
            imag_row = real_row + gc * 8 * tiles
            top = pl.multiple_of(c * 16, 16)
            for j in range(halves * tiles):
                q, h = j // halves, j % halves
                gain_real = wide_ref[h, pl.ds(pl.multiple_of(real_row + q * 8, 8), 8), :]
                gain_imag = wide_ref[h, pl.ds(pl.multiple_of(imag_row + q * 8, 8), 8), :]
                cs, sn = cos_sum[:, j * 128 : (j + 1) * 128], sin_sum[:, j * 128 : (j + 1) * 128]
                model_ref[j, pl.ds(top, 8), :] += gain_real * cs + gain_imag * sn
                model_ref[j, pl.ds(top + 8, 8), :] += gain_imag * cs - gain_real * sn
            return carry

        return lax.fori_loop(0, CHANNELS, channel, carry)

    lax.fori_loop(0, GROUPS, group, 0)

    slot_ref[...] = jnp.zeros_like(slot_ref)
    sample = (lax.broadcasted_iota(jnp.int32, (1, lanes), 1) % TIME).astype(jnp.float32)
    slot = lax.broadcasted_iota(jnp.int32, (WINDOW, lanes), 0).astype(jnp.float32)
    start_row = 2 * gc * 8 * tiles
    inverse_row = start_row + 8 * tiles

    def row_of(row):
        return jnp.concatenate([wide_ref[h, row : row + 1, :] for h in range(halves)], axis=1)

    for sub in range(8 * tiles):
        q, s = sub // 8, sub % 8
        base = pl.multiple_of(base_ref[sub], 128)
        inv = row_of(inverse_row + sub)
        target = (
            row_of(start_row + sub)
            + jnp.floor(sample * inv)
            - base.astype(jnp.float32)
        )
        weight = jnp.where(slot == target, inv, 0.0).astype(jnp.bfloat16)
        values = jnp.concatenate(
            [model_ref[q * halves + h, pl.ds(s, 8, stride=8), :] for h in range(halves)], axis=1
        )
        high = values.astype(jnp.bfloat16).astype(jnp.float32)
        both = jnp.concatenate([high, values - high], axis=0).astype(jnp.bfloat16)
        placed = lax.dot_general(
            both, weight, (((1,), (1,)), ((), ())), preferred_element_type=jnp.float32
        )
        slot_ref[:, pl.ds(base, WINDOW)] += placed[:8] + placed[8:]
    capacity = observed_ref.shape[2]
    for c in range(CHANNELS):
        out_ref[c] = observed_ref[c] - slot_ref[2 * c : 2 * c + 2, :capacity]


def on_device(
    observed,
    baseline_uvw_rows,
    frequencies,
    source_offset,
    source_flux,
    source_group,
    direction_gain,
    station_first,
    station_second,
    average_exponent,
    owner_plan,
):
    owners = lax.axis_size("bl")
    me = lax.axis_index("bl")
    my_dir = lax.axis_index("dir")
    local_channels = observed.shape[0]
    capacity = observed.shape[2]
    block_rows = BLOCK_BASELINES * TIME
    f32 = jnp.float32

    gains = lax.all_to_all(direction_gain[0], "dir", 0, 0, tiled=True)

    send = pl.pallas_call(
        route_kernel,
        out_shape=jax.ShapeDtypeStruct((owners, 3, block_rows), f32),
        in_specs=[SMEM, VMEM],
        out_specs=VMEM,
        name="route",
    )(lax.dynamic_index_in_dim(owner_plan, me, 0, keepdims=False), baseline_uvw_rows)
    arrived = lax.all_to_all(send, "bl", 0, 0, tiled=True)

    mine = (owner_plan == me)[:, :, None]
    per_block = (owners, owners, BLOCK_BASELINES)

    def own(ids):
        return jnp.sum(jnp.where(mine, ids.reshape(per_block), 0), axis=1, dtype=jnp.int32).reshape(-1)

    own_first, own_second, own_exponent = own(station_first), own(station_second), own(average_exponent)
    baselines = own_first.shape[0]
    counts = jnp.right_shift(TIME, own_exponent)
    earlier = jnp.arange(baselines)[:, None] < jnp.arange(baselines)[None, :]
    starts = jnp.sum(jnp.where(earlier, counts[:, None], 0), axis=0, dtype=jnp.int32)
    base = (starts.reshape(-1, SUB)[:, 0] // 128) * 128
    table = jnp.stack([own_first, own_second, starts, counts])

    number = jnp.arange(source_group.shape[0])
    before = (source_group[:, None] == source_group[None, :]) & (number[:, None] < number[None, :])
    place = source_group * PER_GROUP + jnp.sum(before, axis=0, dtype=jnp.int32)
    order = place[:, None] == number[None, :]
    own_flux = lax.dynamic_slice_in_dim(source_flux, my_dir * local_channels, local_channels, 0)
    values = jnp.concatenate([source_offset, own_flux], axis=0)
    values = jnp.sum(jnp.where(order[None], values[:, :, None], 0.0), axis=1)
    east, north = values[0], values[1]
    depth = jnp.sqrt(1.0 - east * east - north * north) - 1.0
    offsets = jnp.stack([east, north, depth])
    flux = values[2:]
    total = jnp.sum(flux.reshape(local_channels, GROUPS, PER_GROUP), axis=2)
    own_freq = lax.dynamic_slice_in_dim(frequencies, my_dir * local_channels, local_channels, 0)

    gc = gains.shape[0]
    tiles = baselines // (8 * SUB)
    lanes = SUB * TIME
    return pl.pallas_call(
        main_kernel,
        out_shape=jax.ShapeDtypeStruct(observed.shape, f32),
        in_specs=[SMEM] * 5 + [VMEM] * 4,
        out_specs=VMEM,
        scratch_shapes=[
            pltpu.VMEM((3, 8, tiles * lanes), f32),
            pltpu.VMEM((lanes // 128, (2 * gc + 16) * 8 * tiles, 128), f32),
            pltpu.VMEM((PER_GROUP, 8, tiles * lanes), f32),
            pltpu.VMEM((tiles * lanes // 128, 2 * CHANNELS * 8, 128), f32),
            pltpu.VMEM((2 * CHANNELS, capacity + WINDOW), f32),
        ],
        compiler_params=pltpu.CompilerParams(vmem_limit_bytes=40 << 20),
        name="predict",
    )(offsets, flux, own_freq, total, base, arrived, gains, table, observed)


def solution(mesh):
    in_specs = (
        P("dir", None, "bl"),
        P(None, "bl"),
        P(),
        P(),
        P(),
        P(),
        P("dir", None, None, None),
        P(),
        P(),
        P(),
        P(),
    )
    return jax.shard_map(
        on_device, mesh=mesh, in_specs=in_specs, out_specs=P("dir", None, "bl"), check_vma=False
    )
```

time: 453 us -> 57.5 us (0.13)
  matrix products: 290 us -> 0 us
  local copies, waits for them, and re-layouts: 66.4 us -> 3.04 us
  loops' own time: 33.9 us -> 0 us
  Pallas kernels: 0 us -> 28.2 us
  waiting for transfers between devices: 27.9 us -> 10.2 us
  other arithmetic: 14.9 us -> 0.97 us
  blocking collectives: 5.45 us -> 0 us
    dot_general x22 -> x0, matrix products: 290 us -> none  [the longest x8 139 us: row_piece(): jnp.einsum('ck,ckr->cr', flux, jnp.sin(angles), precision=lax.Precision.H...]
    another operation x2 -> x0, loops' own time: 33.9 us -> none  [the longest x1 33.7 us: pack_pieces(): buffer = lax.fori_loop(0, piece_count, place_piece, buffer)]
    pallas_call x0 -> x2, Pallas kernels: none -> 28.2 us  [the longest x1 26.7 us: on_device(): pl.pallas_call(main_kernel, out_shape=jax.ShapeDtypeStruct(observed.shape...]
    all_to_all x2, waiting for transfers between devices: 27.9 us -> 10.2 us  [the longest x1 5.21 us: on_device(): arrived = lax.all_to_all(send, 'bl', 0, 0, tiled=True)]
    reshape x7 -> x5, local copies, waits for them, and re-layouts: 16.9 us -> 0.39 us  [the longest x3 0.24 us: own(): ids.reshape(per_block)]
    dynamic_update_slice x16 -> x0, local copies, waits for them, and re-layouts: 13.3 us -> none  [place_piece(): return lax.dynamic_update_slice_in_dim(current, piece, starts[index], 2)]
    dynamic_slice x19 -> x2, local copies, waits for them, and re-layouts: 12.3 us -> 0.09 us  [the longest x1 0.07 us: on_device(): lax.dynamic_slice_in_dim(frequencies, my_dir * local_channels, local_chan...]
    broadcast_in_dim x4 -> x0, local copies, waits for them, and re-layouts: 9.27 us -> none  [the longest x1 4.55 us: predict_rows(): gain_real = jnp.repeat(gain_real, TIME_SAMPLES, axis=1)]
  transfers between devices with their start and end apart: 2 -> 2, of which waited for: 2 -> 2; matrix products, arithmetic and copies ran while one was open for 1% -> 3% of each run, Pallas kernels for 0% -> 0%
where the time goes in v1:
time: 57.5 us; the launch traced here: 56.5 us
  Pallas kernels  28.2 us (49%)
  starting transfers between devices  13.9 us (24%)
  waiting for transfers between devices  10.2 us (18%)
  local copies, waits for them, and re-layouts  3.04 us (5%)
  other arithmetic  0.97 us (2%)
    pallas_call x1, Pallas kernels, on_device(): pl.pallas_call(main_kernel, out_shape=jax.ShapeDtypeStruct(observed.shape...  26.7 us
    all_to_all x1, starting transfers between devices, on_device(): arrived = lax.all_to_all(send, 'bl', 0, 0, tiled=True)  8.58 us
    all_to_all x1, starting transfers between devices, on_device(): gains = lax.all_to_all(direction_gain[0], 'dir', 0, 0, tiled=True)  5.28 us
    all_to_all x1, waiting for transfers between devices, on_device(): arrived = lax.all_to_all(send, 'bl', 0, 0, tiled=True)  5.21 us
    all_to_all x1, waiting for transfers between devices, on_device(): gains = lax.all_to_all(direction_gain[0], 'dir', 0, 0, tiled=True)  5.04 us
    pallas_call x1, Pallas kernels, on_device(): pl.pallas_call(route_kernel, out_shape=jax.ShapeDtypeStruct((owners, 3, b...  1.56 us
    squeeze x1, local copies, waits for them, and re-layouts, on_device(): lax.dynamic_index_in_dim(owner_plan, me, 0, keepdims=False)  1.21 us
  transfers between devices with their start and end apart: 2, of which 2 were waited for; matrix products, arithmetic and copies ran while one was open for 3% of the time, Pallas kernels for 0%

profile of v1, /device:TPU:1, one launch (start us, length us, event | category | flops | bytes accessed | tf_op | source)
XLA Modules:
  0.0 56.5 jit_solution(5265841669787069030)
XLA Ops:
  0.0 1.2 %dynamic-slice_bitcast_fusion.plan_ref = s32[16]{0:T(128)} fusion(s32[16,16]{1,0:T(8,128)} %param.21, s32[]{:T(128)S(6)} %select_n.36), kind=kLoop, calls=%fused_computation.26 | loop fusion | bytes 132 | tf_op jit(solution)/shard_map/jit(dynamic_index_in_dim)/squeeze | solution.py:222
  1.2 1.6 %route.1 = f32[16,3,512]{2,1,0:T(4,128)} custom-call(s32[16]{0:T(128)} %dynamic-slice_bitcast_fusion.plan_ref, f32[3,8192]{1,0:T(4,128)} %uvw_ref.1), custom_call_target="tpu_custom_call" | custom-call | tf_op jit(solution)/shard_map/route/pallas_call | solution.py:216
  2.8 8.6 %all-to-all-start = ((f32[16,3,512]{2,1,0:T(4,128)}), f32[16,3,512]{2,1,0:T(4,128)S(1)}, u32[]{:S(2)}, u32[]{:S(2)}) async-start(f32[16,3,512]{2,1,0:T(4,128)} %route.1), calls=%async_computation | async-start | bytes 262144 | tf_op jit(solution)/shard_map/all_to_all | solution.py:223
  11.4 0.0 copy-start.3
  11.4 0.0 copy-done.2
  11.4 0.0 copy-start.4
  11.4 0.1 reshape.58
  11.5 0.6 %copy-done.3 = s32[8192]{0:T(1024)S(1)} copy-done((s32[8192]{0:T(1024)S(1)}, s32[8192]{0:T(1024)}, u32[]{:S(2)}) %copy-start.3) | copy-done | bytes 32792
  12.1 0.1 reshape.60
  12.2 0.0 copy-done.4
  12.2 0.1 reshape.61
  12.3 0.0 copy-start.5
  12.3 0.0 copy-start.7
  12.3 0.2 select_reduce_fusion.3
  12.5 0.1 shift_right_arithmetic.25
  12.6 0.2 select_reduce_fusion.1
  12.7 0.3 copy-done.5
  13.0 0.1 convert_reduce_fusion
  13.1 0.1 iota_compare_fusion.1
  13.3 0.3 select_reduce_fusion
  13.6 0.1 reshape.59
  13.7 0.1 slice_reduce_fusion
  13.8 5.2 %all-to-all-done.uvw_ref = f32[16,3,512]{2,1,0:T(4,128)S(1)} async-done(((f32[16,3,512]{2,1,0:T(4,128)}), f32[16,3,512]{2,1,0:T(4,128)S(1)}, u32[]{:S(2)}, u32[]{:S(2)}) %all-to-all-start) | async-done | bytes 98336 | tf_op jit(solution)/shard_map/all_to_all | solution.py:223
  19.0 5.3 %all-to-all-start.1 = ((f32[32,2,512]{2,1,0:T(2,128)}), f32[32,2,512]{2,1,0:T(2,128)S(1)}, u32[]{:S(2)}, u32[]{:S(2)}) async-start(f32[32,2,512]{2,1,0:T(2,128)} %bitcast.1), calls=%async_computation.1 | async-start | bytes 262144 | tf_op jit(solution)/shard_map/all_to_all | solution.py:214
  24.3 0.1 shift_right_arithmetic.26
  24.4 0.1 stack_reshape.6
  24.5 0.1 stack_reshape.7
  24.6 0.1 reshape.57
  24.6 0.1 dynamic_slice.11.freq_ref
  24.7 0.1 reduce_sum.65.total_ref
  24.8 5.0 %all-to-all-done.1.gain_ref = f32[32,2,512]{2,1,0:T(2,128)S(1)} async-done(((f32[32,2,512]{2,1,0:T(2,128)}), f32[32,2,512]{2,1,0:T(2,128)S(1)}, u32[]{:S(2)}, u32[]{:S(2)}) %all-to-all-start.1) | async-done | bytes 131104 | tf_op jit(solution)/shard_map/all_to_all | solution.py:214
  29.9 26.7 %predict.1 = f32[4,2,3840]{2,1,0:T(2,128)} custom-call(f32[3,256]{1,0:T(4,128)S(1)} %pad_maximum_fusion.1.offset_ref, f32[4,256]{1,0:T(4,128)S(1)} %slice.23.flux_ref, f32[4]{0:T(128)S(1)} %dynamic_slice.11.freq_ref, f32[4,8]{1,0:T(4,128)S(1)} %reduce_sum.65.total_ref, s32[32]{0:T(128)S(1)} %fusion.3.base_ref, f32[16,3,512]{2,1,0:T(4,128)S(1)} %all-to-all-done.uvw_ref, ...), custom_call_target="tpu_custom_call" | custom-call | tf_op jit(solution)/shard_map/predict/pallas_call | solution.py:256
  (21 shorter events, 0.1 us)
Async XLA Ops:
  0.0 13.2 %copy-start = (f32[32,256]{1,0:T(8,128)S(1)}, f32[32,256]{1,0:T(8,128)}, u32[]{:S(2)}) copy-start(f32[32,256]{1,0:T(8,128)} %param.15) | copy-start | bytes 98308
  2.8 8.6 %copy-start.6 = (s32[16,16]{1,0:T(8,128)S(1)}, s32[16,16]{1,0:T(8,128)}, u32[]{:S(2)}) copy-start(s32[16,16]{1,0:T(8,128)} %param.21) | copy-start | bytes 3076
  2.8 8.6 %copy-start.2 = (s32[8192]{0:T(1024)S(1)}, s32[8192]{0:T(1024)}, u32[]{:S(2)}) copy-start(s32[8192]{0:T(1024)} %param.20) | copy-start | bytes 98308
  2.8 16.3 %all-to-all-start = ((f32[16,3,512]{2,1,0:T(4,128)}), f32[16,3,512]{2,1,0:T(4,128)S(1)}, u32[]{:S(2)}, u32[]{:S(2)}) async-start(f32[16,3,512]{2,1,0:T(4,128)} %route.1), calls=%async_computation | async-start | bytes 262144 | tf_op jit(solution)/shard_map/all_to_all | solution.py:223
  11.4 0.8 %copy-start.3 = (s32[8192]{0:T(1024)S(1)}, s32[8192]{0:T(1024)}, u32[]{:S(2)}) copy-start(s32[8192]{0:T(1024)} %param.18) | copy-start | bytes 98308
  11.4 0.8 %copy-start.4 = (s32[8192]{0:T(1024)S(1)}, s32[8192]{0:T(1024)}, u32[]{:S(2)}) copy-start(s32[8192]{0:T(1024)} %param.19) | copy-start | bytes 98308
  12.3 0.7 %copy-start.5 = (s32[256]{0:T(256)S(1)}, s32[256]{0:T(256)}, u32[]{:S(2)}) copy-start(s32[256]{0:T(256)} %param.16) | copy-start | bytes 3076
  12.3 0.9 %copy-start.7 = (f32[2,256]{1,0:T(2,128)S(1)}, f32[2,256]{1,0:T(2,128)}, u32[]{:S(2)}) copy-start(f32[2,256]{1,0:T(2,128)} %param.14) | copy-start | bytes 6148
  19.0 5.6 %copy-start.8 = (f32[32]{0:T(128)S(1)}, f32[32]{0:T(128)}, u32[]{:S(2)}) copy-start(f32[32]{0:T(128)} %param.13) | copy-start | bytes 388
  19.0 10.8 %copy-start.1 = (f32[4,2,3840]{2,1,0:T(2,128)S(1)}, f32[4,2,3840]{2,1,0:T(2,128)}, u32[]{:S(2)}) copy-start(f32[4,2,3840]{2,1,0:T(2,128)} %observed_ref.1) | copy-start | bytes 368644
  19.0 10.8 %all-to-all-start.1 = ((f32[32,2,512]{2,1,0:T(2,128)}), f32[32,2,512]{2,1,0:T(2,128)S(1)}, u32[]{:S(2)}, u32[]{:S(2)}) async-start(f32[32,2,512]{2,1,0:T(2,128)} %bitcast.1), calls=%async_computation.1 | async-start | bytes 262144 | tf_op jit(solution)/shard_map/all_to_all | solution.py:214

commit v2 on v1

--- a/solution.py
+++ b/solution.py
@@ -33,11 +33,15 @@
     return high, middle, low
 
 
-def route_kernel(plan_ref, uvw_ref, out_ref):
-    owners = out_ref.shape[0]
-    rows = out_ref.shape[2]
-    for k in range(owners):
-        out_ref[plan_ref[k]] = uvw_ref[:, k * rows : (k + 1) * rows]
+def route_kernel(plan_ref, uvw_ref, gain_ref, out_ref):
+    my_dir, me = lax.axis_index("dir"), lax.axis_index("bl")
+    members, _, rows = out_ref.shape
+    for k in range(members):
+        out_ref[plan_ref[me, k], :3] = uvw_ref[:, k * rows : (k + 1) * rows]
+    for j in range(members):
+        its_dir = lax.rem(my_dir - me // 2 + j // 2 + GROUPS, GROUPS)
+        gains = gain_ref[pl.ds(its_dir * CHANNELS, CHANNELS)]
+        out_ref[j, 4:] = jnp.where(me % 2 == 0, gains[:, 0, :], gains[:, 1, :])
 
 
 def main_kernel(
@@ -46,22 +50,23 @@
     freq_ref,
     total_ref,
     base_ref,
-    uvw_ref,
-    gain_ref,
     table_ref,
     observed_ref,
+    arrived_ref,
     out_ref,
     u_ref,
     wide_ref,
     x_ref,
     model_ref,
     slot_ref,
+    gain_ref,
+    narrow_ref,
+    staged_ref,
 ):
-    sources = uvw_ref.shape[0]
-    baselines = gain_ref.shape[2]
-    stations = gain_ref.shape[2]
-    gc = gain_ref.shape[0]
-    rows_of = 2 * gc + 16
+    sources, _, stations = arrived_ref.shape
+    baselines = table_ref.shape[1]
+    gc = GROUPS * CHANNELS
+    rows_of = 2 * gc + 8
     lanes = SUB * TIME
     tiles = baselines // (8 * SUB)
     halves = lanes // 128
@@ -71,48 +76,66 @@
             sub = 2 * p + half
             q, s = sub // 8, sub % 8
             for d in range(3):
-                u_ref[d, s : s + 1, q * lanes : (q + 1) * lanes] = uvw_ref[
+                u_ref[d, s : s + 1, q * lanes : (q + 1) * lanes] = arrived_ref[
                     p, d : d + 1, half * lanes : (half + 1) * lanes
                 ]
 
-    gain_rows = jnp.concatenate([gain_ref[:, 0, :], gain_ref[:, 1, :]], axis=0)
-    pieces = jnp.concatenate(split3(gain_rows), axis=0)
+    for j in range(GROUPS):
+        g = lax.rem(lax.axis_index("dir") - lax.axis_index("bl") // 2 + j + GROUPS, GROUPS)
+        gain_ref[pl.ds(pl.multiple_of(g * 8, 8), 8)] = jnp.concatenate(
+            [arrived_ref[2 * j, 4:], arrived_ref[2 * j + 1, 4:]], axis=0
+        )
+    pieces = jnp.concatenate(split3(gain_ref[...]), axis=0)
     station = lax.broadcasted_iota(jnp.int32, (stations, baselines), 0)
 
     def picked(row):
         ids = table_ref[row : row + 1, :]
-        one_hot = (station == ids).astype(jnp.float32).astype(jnp.bfloat16)
+        one_hot = jnp.where(station == ids, 1.0, 0.0).astype(jnp.bfloat16)
         found = jnp.dot(pieces, one_hot, preferred_element_type=jnp.float32)
         n = 2 * gc
         return found[:n] + found[n : 2 * n] + found[2 * n :]
 
     first = picked(0)
     second = picked(1)
-    pair_real = first[:gc] * second[:gc] + first[gc:] * second[gc:]
-    pair_imag = first[gc:] * second[:gc] - first[:gc] * second[gc:]
+    def swapped(rows):
+        return pltpu.roll(rows.reshape(GROUPS, 8, baselines), 4, 1).reshape(2 * gc, baselines)
+
+    straight = first * second
+    crossed = first * swapped(second)
+    part = lax.broadcasted_iota(jnp.int32, (2 * gc, baselines), 0) & CHANNELS
+    pair = jnp.where(part == 0, straight + swapped(straight), crossed - swapped(crossed))
     starts = table_ref[2:3, :].astype(jnp.float32)
     inverse = table_ref[3:4, :].astype(jnp.float32) * (1.0 / TIME)
     narrow = jnp.concatenate(
-        [pair_real, pair_imag, starts, inverse, jnp.zeros((14, baselines), jnp.float32)], axis=0
+        [pair, starts, inverse, jnp.zeros((6, baselines), jnp.float32)], axis=0
     )
-    narrow = jnp.concatenate(split3(narrow), axis=0)
+    high = narrow.astype(jnp.bfloat16).astype(jnp.float32)
+    narrow_ref[0] = high
+    narrow_ref[1] = narrow - high
     per_tile = 8 * SUB
-    width = per_tile * TIME
-    spread = (
-        lax.broadcasted_iota(jnp.int32, (per_tile, width), 0)
-        == lax.broadcasted_iota(jnp.int32, (per_tile, width), 1) // TIME
-    ).astype(jnp.float32).astype(jnp.bfloat16)
+    spread = jnp.where(
+        lax.broadcasted_iota(jnp.int32, (per_tile, lanes), 0) & (SUB - 1)
+        == lax.shift_right_logical(lax.broadcasted_iota(jnp.int32, (per_tile, lanes), 1), 4),
+        1.0,
+        0.0,
+    ).astype(jnp.bfloat16)
+    spread = jnp.concatenate([spread, spread], axis=0)
+    in_sublane = jnp.where(
+        lax.broadcasted_iota(jnp.int32, (8, per_tile), 0)
+        == lax.shift_right_logical(lax.broadcasted_iota(jnp.int32, (8, per_tile), 1), 4),
+        1.0,
+        0.0,
+    )
     for q in range(tiles):
-        wide = jnp.dot(
-            narrow[:, q * per_tile : (q + 1) * per_tile], spread, preferred_element_type=jnp.float32
-        )
-        wide = wide[:rows_of] + wide[rows_of : 2 * rows_of] + wide[2 * rows_of :]
-        for s in range(8):
-            for h in range(halves):
-                left = s * lanes + h * 128
-                wide_ref[h, pl.ds(q * 8 + s, rows_of, stride=8 * tiles), :] = wide[
-                    :, left : left + 128
-                ]
+        at = slice(q * per_tile, (q + 1) * per_tile)
+        for r in range(rows_of):
+            for part in range(2):
+                staged_ref[r * 8 : r * 8 + 8, part * per_tile : (part + 1) * per_tile] = (
+                    narrow_ref[part, r : r + 1, at] * in_sublane
+                )
+        wide_ref[q] = jnp.dot(
+            staged_ref[...].astype(jnp.bfloat16), spread, preferred_element_type=jnp.float32
+        )
 
     model_ref[...] = jnp.zeros_like(model_ref)
 
@@ -141,13 +164,14 @@
                 b = b + w * tangent
             cos_sum = (2.0 * SCALE) * a - total_ref[c, g]
             sin_sum = (2.0 * SCALE**0.5) * b
-            real_row = (g * CHANNELS + c) * 8 * tiles
-            imag_row = real_row + gc * 8 * tiles
+            real_row = pl.multiple_of((g * 2 * CHANNELS + c) * 8, 8)
+            imag_row = pl.multiple_of(real_row + CHANNELS * 8, 8)
             top = pl.multiple_of(c * 16, 16)
             for j in range(halves * tiles):
                 q, h = j // halves, j % halves
-                gain_real = wide_ref[h, pl.ds(pl.multiple_of(real_row + q * 8, 8), 8), :]
-                gain_imag = wide_ref[h, pl.ds(pl.multiple_of(imag_row + q * 8, 8), 8), :]
+                lane = slice(h * 128, (h + 1) * 128)
+                gain_real = wide_ref[q, pl.ds(real_row, 8), lane]
+                gain_imag = wide_ref[q, pl.ds(imag_row, 8), lane]
                 cs, sn = cos_sum[:, j * 128 : (j + 1) * 128], sin_sum[:, j * 128 : (j + 1) * 128]
                 model_ref[j, pl.ds(top, 8), :] += gain_real * cs + gain_imag * sn
                 model_ref[j, pl.ds(top + 8, 8), :] += gain_imag * cs - gain_real * sn
@@ -158,20 +182,16 @@
     lax.fori_loop(0, GROUPS, group, 0)
 
     slot_ref[...] = jnp.zeros_like(slot_ref)
-    sample = (lax.broadcasted_iota(jnp.int32, (1, lanes), 1) % TIME).astype(jnp.float32)
+    sample = (lax.broadcasted_iota(jnp.int32, (1, lanes), 1) & (TIME - 1)).astype(jnp.float32)
     slot = lax.broadcasted_iota(jnp.int32, (WINDOW, lanes), 0).astype(jnp.float32)
-    start_row = 2 * gc * 8 * tiles
-    inverse_row = start_row + 8 * tiles
-
-    def row_of(row):
-        return jnp.concatenate([wide_ref[h, row : row + 1, :] for h in range(halves)], axis=1)
-
+    start_row = 2 * gc * 8
+    inverse_row = start_row + 8
     for sub in range(8 * tiles):
         q, s = sub // 8, sub % 8
         base = pl.multiple_of(base_ref[sub], 128)
-        inv = row_of(inverse_row + sub)
+        inv = wide_ref[q, inverse_row + s : inverse_row + s + 1, :]
         target = (
-            row_of(start_row + sub)
+            wide_ref[q, start_row + s : start_row + s + 1, :]
             + jnp.floor(sample * inv)
             - base.astype(jnp.float32)
         )
@@ -211,30 +231,31 @@
     block_rows = BLOCK_BASELINES * TIME
     f32 = jnp.float32
 
-    gains = lax.all_to_all(direction_gain[0], "dir", 0, 0, tiled=True)
-
     send = pl.pallas_call(
         route_kernel,
-        out_shape=jax.ShapeDtypeStruct((owners, 3, block_rows), f32),
-        in_specs=[SMEM, VMEM],
+        out_shape=jax.ShapeDtypeStruct((owners, 8, block_rows), f32),
+        in_specs=[SMEM, VMEM, VMEM],
         out_specs=VMEM,
         name="route",
-    )(lax.dynamic_index_in_dim(owner_plan, me, 0, keepdims=False), baseline_uvw_rows)
-    arrived = lax.all_to_all(send, "bl", 0, 0, tiled=True)
+    )(owner_plan, baseline_uvw_rows, direction_gain[0])
+    rings = [[(p // 2 + r) % GROUPS * owners + p for p in range(owners)] for r in range(GROUPS)]
+    arrived = lax.all_to_all(send, ("dir", "bl"), 0, 0, axis_index_groups=rings, tiled=True)
 
     mine = (owner_plan == me)[:, :, None]
     per_block = (owners, owners, BLOCK_BASELINES)
 
     def own(ids):
-        return jnp.sum(jnp.where(mine, ids.reshape(per_block), 0), axis=1, dtype=jnp.int32).reshape(-1)
+        held = jnp.sum(jnp.where(mine, ids.reshape(per_block), 0), axis=1, dtype=jnp.int32)
+        return held
 
     own_first, own_second, own_exponent = own(station_first), own(station_second), own(average_exponent)
-    baselines = own_first.shape[0]
-    counts = jnp.right_shift(TIME, own_exponent)
+    baselines = own_first.size
+    counts = jnp.right_shift(TIME, own_exponent).reshape(-1)
     earlier = jnp.arange(baselines)[:, None] < jnp.arange(baselines)[None, :]
     starts = jnp.sum(jnp.where(earlier, counts[:, None], 0), axis=0, dtype=jnp.int32)
-    base = (starts.reshape(-1, SUB)[:, 0] // 128) * 128
-    table = jnp.stack([own_first, own_second, starts, counts])
+    held = (own_first, own_second, starts.reshape(owners, -1), counts.reshape(owners, -1))
+    table = jnp.stack([h.reshape(-1) for h in held])
+    base = (table[2].reshape(-1, SUB)[:, 0] // 128) * 128
 
     number = jnp.arange(source_group.shape[0])
     before = (source_group[:, None] == source_group[None, :]) & (number[:, None] < number[None, :])
@@ -250,24 +271,27 @@
     total = jnp.sum(flux.reshape(local_channels, GROUPS, PER_GROUP), axis=2)
     own_freq = lax.dynamic_slice_in_dim(frequencies, my_dir * local_channels, local_channels, 0)
 
-    gc = gains.shape[0]
+    gc = GROUPS * local_channels
     tiles = baselines // (8 * SUB)
     lanes = SUB * TIME
     return pl.pallas_call(
         main_kernel,
         out_shape=jax.ShapeDtypeStruct(observed.shape, f32),
-        in_specs=[SMEM] * 5 + [VMEM] * 4,
+        in_specs=[SMEM] * 5 + [VMEM] * 3,
         out_specs=VMEM,
         scratch_shapes=[
             pltpu.VMEM((3, 8, tiles * lanes), f32),
-            pltpu.VMEM((lanes // 128, (2 * gc + 16) * 8 * tiles, 128), f32),
+            pltpu.VMEM((tiles, (2 * gc + 8) * 8, lanes), f32),
             pltpu.VMEM((PER_GROUP, 8, tiles * lanes), f32),
             pltpu.VMEM((tiles * lanes // 128, 2 * CHANNELS * 8, 128), f32),
             pltpu.VMEM((2 * CHANNELS, capacity + WINDOW), f32),
+            pltpu.VMEM((2 * gc, direction_gain.shape[3]), f32),
+            pltpu.VMEM((2, 2 * gc + 8, baselines), f32),
+            pltpu.VMEM(((2 * gc + 8) * 8, 16 * SUB), f32),
         ],
         compiler_params=pltpu.CompilerParams(vmem_limit_bytes=40 << 20),
         name="predict",
-    )(offsets, flux, own_freq, total, base, arrived, gains, table, observed)
+    )(offsets, flux, own_freq, total, base, table, observed, arrived)
 
 
 def solution(mesh):

time: 57.5 us -> 50 us (0.87)
  starting transfers between devices: 13.9 us -> 11.7 us
  local copies, waits for them, and re-layouts: 3.04 us -> 1.01 us
  waiting for transfers between devices: 10.2 us -> 8.83 us
  Pallas kernels: 28.2 us -> 26.9 us
    all_to_all x2 -> x1, starting transfers between devices: 13.9 us -> 11.7 us  [on_device(): lax.all_to_all(send, ('dir', 'bl'), 0, 0, axis_index_groups=rings, tiled=...]
    pallas_call x1, Pallas kernels: 26.7 us -> 25.1 us  [on_device(): pl.pallas_call(main_kernel, out_shape=jax.ShapeDtypeStruct(observed.shape...]
    all_to_all x2 -> x1, waiting for transfers between devices: 10.2 us -> 8.83 us  [on_device(): lax.all_to_all(send, ('dir', 'bl'), 0, 0, axis_index_groups=rings, tiled=...]
    squeeze x1 -> x0, local copies, waits for them, and re-layouts: 1.21 us -> none  [on_device(): lax.dynamic_index_in_dim(owner_plan, me, 0, keepdims=False)]
    unnamed x18, local copies, waits for them, and re-layouts: 0.92 us -> 0.08 us
  transfers between devices with their start and end apart: 2 -> 1, of which waited for: 2 -> 1; matrix products, arithmetic and copies ran while one was open for 3% -> 4% of each run, Pallas kernels for 0% -> 0%
where the time goes in v2:
time: 50 us; the launch traced here: 49.6 us
  Pallas kernels  26.9 us (54%)
  starting transfers between devices  11.7 us (23%)
  waiting for transfers between devices  8.83 us (18%)
  local copies, waits for them, and re-layouts  1.01 us (2%)
  other arithmetic  0.97 us (2%)
    pallas_call x1, Pallas kernels, on_device(): pl.pallas_call(main_kernel, out_shape=jax.ShapeDtypeStruct(observed.shape...  25.1 us
    all_to_all x1, starting transfers between devices, on_device(): lax.all_to_all(send, ('dir', 'bl'), 0, 0, axis_index_groups=rings, tiled=...  11.7 us
    all_to_all x1, waiting for transfers between devices, on_device(): lax.all_to_all(send, ('dir', 'bl'), 0, 0, axis_index_groups=rings, tiled=...  8.83 us
    pallas_call x1, Pallas kernels, on_device(): pl.pallas_call(route_kernel, out_shape=jax.ShapeDtypeStruct((owners, 8, b...  1.76 us
  transfers between devices with their start and end apart: 1, of which 1 were waited for; matrix products, arithmetic and copies ran while one was open for 4% of the time, Pallas kernels for 0%

profile of v2, /device:TPU:1, one launch (start us, length us, event | category | flops | bytes accessed | tf_op | source)
XLA Modules:
  0.0 49.6 jit_solution(16683880756985499663)
XLA Ops:
  0.0 0.0 copy-start
  0.0 1.8 %route.1 = f32[16,8,512]{2,1,0:T(8,128)} custom-call(s32[16,16]{1,0:T(8,128)} %plan_ref.1, f32[3,8192]{1,0:T(4,128)} %uvw_ref.1, f32[32,2,512]{2,1,0:T(2,128)} %bitcast.2), custom_call_target="tpu_custom_call" | custom-call | tf_op jit(solution)/shard_map/route/pallas_call | solution.py:234
  1.8 11.7 %all-to-all-start = ((f32[16,8,512]{2,1,0:T(8,128)}), f32[16,8,512]{2,1,0:T(8,128)S(1)}, u32[]{:S(2)}, u32[]{:S(2)}) async-start(f32[16,8,512]{2,1,0:T(8,128)} %route.1), calls=%async_computation | async-start | bytes 524288 | tf_op jit(solution)/shard_map/all_to_all | solution.py:242
  13.5 0.0 copy-done.6
  13.5 0.1 convert_reduce_fusion
  13.6 0.0 copy-start.5
  13.7 0.1 iota_compare_fusion.1
  13.8 0.0 copy-done
  13.8 0.0 copy-done.7
  13.8 0.3 select_reduce_fusion
  14.1 0.0 copy-done.2
  14.2 0.0 copy-done.3
  14.2 0.1 reshape.55
  14.3 0.0 copy-done.4
  14.3 0.1 reshape.56
  14.4 0.0 copy-done.5
  14.4 0.1 reshape.54
  14.5 0.0 copy-start.8
  14.5 0.0 copy-start.1
  14.5 0.2 select_reduce_fusion.3
  14.7 0.1 shift_right_arithmetic.26
  14.8 0.1 shift_right_arithmetic.25
  14.9 0.1 stack_reshape.6
  14.9 0.1 stack_reshape.7
  15.0 0.1 select_reduce_fusion.1
  15.2 0.1 reshape_squeeze_stack_reshape_reshape.3
  15.2 0.1 slice_reduce_fusion
  15.4 0.1 dynamic_slice.7.freq_ref
  15.5 0.1 reshape.53
  15.6 0.1 reduce_sum.65.total_ref
  15.7 8.8 %all-to-all-done.arrived_ref = f32[16,8,512]{2,1,0:T(8,128)S(1)} async-done(((f32[16,8,512]{2,1,0:T(8,128)}), f32[16,8,512]{2,1,0:T(8,128)S(1)}, u32[]{:S(2)}, u32[]{:S(2)}) %all-to-all-start) | async-done | bytes 262176 | tf_op jit(solution)/shard_map/all_to_all | solution.py:242
  24.5 25.1 %predict.1 = f32[4,2,3840]{2,1,0:T(2,128)} custom-call(f32[3,256]{1,0:T(4,128)S(1)} %pad_maximum_fusion.1.offset_ref, f32[4,256]{1,0:T(4,128)S(1)} %slice.23.flux_ref, f32[4]{0:T(128)S(1)} %dynamic_slice.7.freq_ref, f32[4,8]{1,0:T(4,128)S(1)} %reduce_sum.65.total_ref, s32[32]{0:T(128)S(1)} %fusion.3.base_ref, s32[4,512]{1,0:T(4,128)S(1)} %pad_add_fusion.table_ref, ...), custom_call_target="tpu_custom_call" | custom-call | tf_op jit(solution)/shard_map/predict/pallas_call | solution.py:277
  (18 shorter events, 0.1 us)
Async XLA Ops:
  0.0 13.8 %copy-start = (f32[32,256]{1,0:T(8,128)S(1)}, f32[32,256]{1,0:T(8,128)}, u32[]{:S(2)}) copy-start(f32[32,256]{1,0:T(8,128)} %param.15) | copy-start | bytes 98308
  1.8 11.8 %copy-start.6 = (s32[256]{0:T(256)S(1)}, s32[256]{0:T(256)}, u32[]{:S(2)}) copy-start(s32[256]{0:T(256)} %param.16) | copy-start | bytes 3076
  1.8 12.0 %copy-start.7 = (f32[2,256]{1,0:T(2,128)S(1)}, f32[2,256]{1,0:T(2,128)}, u32[]{:S(2)}) copy-start(f32[2,256]{1,0:T(2,128)} %param.14) | copy-start | bytes 6148
  1.8 12.4 %copy-start.2 = (s32[16,16]{1,0:T(8,128)S(1)}, s32[16,16]{1,0:T(8,128)}, u32[]{:S(2)}) copy-start(s32[16,16]{1,0:T(8,128)} %plan_ref.1) | copy-start | bytes 3076
  1.8 12.4 %copy-start.3 = (s32[8192]{0:T(1024)S(1)}, s32[8192]{0:T(1024)}, u32[]{:S(2)}) copy-start(s32[8192]{0:T(1024)} %param.18) | copy-start | bytes 98308
  1.8 22.7 %all-to-all-start = ((f32[16,8,512]{2,1,0:T(8,128)}), f32[16,8,512]{2,1,0:T(8,128)S(1)}, u32[]{:S(2)}, u32[]{:S(2)}) async-start(f32[16,8,512]{2,1,0:T(8,128)} %route.1), calls=%async_computation | async-start | bytes 524288 | tf_op jit(solution)/shard_map/all_to_all | solution.py:242
  13.5 0.8 %copy-start.4 = (s32[8192]{0:T(1024)S(1)}, s32[8192]{0:T(1024)}, u32[]{:S(2)}) copy-start(s32[8192]{0:T(1024)} %param.19) | copy-start | bytes 98308
  13.6 0.8 %copy-start.5 = (s32[8192]{0:T(1024)S(1)}, s32[8192]{0:T(1024)}, u32[]{:S(2)}) copy-start(s32[8192]{0:T(1024)} %param.20) | copy-start | bytes 98308
  14.5 0.9 %copy-start.8 = (f32[32]{0:T(128)S(1)}, f32[32]{0:T(128)}, u32[]{:S(2)}) copy-start(f32[32]{0:T(128)} %param.13) | copy-start | bytes 388
  14.5 10.0 %copy-start.1 = (f32[4,2,3840]{2,1,0:T(2,128)S(1)}, f32[4,2,3840]{2,1,0:T(2,128)}, u32[]{:S(2)}) copy-start(f32[4,2,3840]{2,1,0:T(2,128)} %observed_ref.1) | copy-start | bytes 368644

commit v3 on v2

v3 whole, which is shorter than its diff:
```python
import functools

import jax
import jax.numpy as jnp
from jax import lax
from jax.experimental import pallas as pl
from jax.experimental.pallas import tpu as pltpu
from jax.sharding import PartitionSpec as P


TIME = 16
GROUPS = 8
PER_GROUP = 32
CHANNELS = 4
BLOCK_BASELINES = 32
SUB = 16
WINDOW = 384

POLE = 0.2500051432960012
LINE0 = 0.9326632751760481
LINE1 = 0.23550642249107842
SCALE = 2.4653076166502004

VMEM = pl.BlockSpec(memory_space=pltpu.VMEM)
SMEM = pl.BlockSpec(memory_space=pltpu.SMEM)


def split3(values):
    high = values.astype(jnp.bfloat16)
    rest = values - high.astype(jnp.float32)
    middle = rest.astype(jnp.bfloat16)
    low = (rest - middle.astype(jnp.float32)).astype(jnp.bfloat16)
    return high, middle, low


def route_kernel(plan_ref, uvw_ref, out_ref):
    me = lax.axis_index("bl")
    owners, _, rows = out_ref.shape
    for k in range(owners):
        out_ref[plan_ref[me, k]] = uvw_ref[:, k * rows : (k + 1) * rows]


def sums_kernel(
    offset_ref, flux_ref, freq_ref, total_ref, arrived_ref, sums_ref, u_ref, x_ref
):
    sources, _, rows = arrived_ref.shape
    lanes = SUB * TIME
    width = u_ref.shape[2]

    for p in range(sources):
        for half in range(2):
            sub = 2 * p + half
            q, s = sub // 8, sub % 8
            for d in range(3):
                u_ref[d, s : s + 1, q * lanes : (q + 1) * lanes] = arrived_ref[
                    p, d : d + 1, half * lanes : (half + 1) * lanes
                ]
    def group(g, carry):
        for h in range(2):
            at = slice(h * (width) // 2, (h + 1) * (width) // 2)
            u, v, w = u_ref[0, :, at], u_ref[1, :, at], u_ref[2, :, at]
            for k in range(PER_GROUP):
                i = g * PER_GROUP + k
                x_ref[k, :, at] = u * offset_ref[0, i] + v * offset_ref[1, i] + w * offset_ref[2, i]

        def channel(c, ratio):
            a = jnp.zeros((8, width), jnp.float32)
            b = jnp.zeros((8, width), jnp.float32)
            for k in range(PER_GROUP):
                y = x_ref[k] if ratio is None else x_ref[k] * ratio
                t = y - jnp.round(y)
                q = t * t
                tangent = t * (pltpu.reciprocal(POLE - q, approx=True) + (LINE1 * q + LINE0))
                w = flux_ref[c, g * PER_GROUP + k] * pltpu.reciprocal(
                    tangent * tangent + SCALE, approx=True
                )
                a = a + w
                b = b + w * tangent
            cos_sum = (2.0 * SCALE) * a - total_ref[c, g]
            sin_sum = (2.0 * SCALE**0.5) * b
            sums_ref[0, g * CHANNELS + c] = cos_sum
            sums_ref[1, g * CHANNELS + c] = sin_sum

        channel(0, None)

        def other(c, carry):
            channel(c, freq_ref[c])
            return carry

        return lax.fori_loop(1, CHANNELS, other, carry)

    lax.fori_loop(0, GROUPS, group, 0)


def finish_kernel(
    base_ref,
    table_ref,
    observed_ref,
    sums_ref,
    arrived_ref,
    out_ref,
    wide_ref,
    model_ref,
    slot_ref,
    gain_ref,
    narrow_ref,
    staged_ref,
):
    stations = arrived_ref.shape[2]
    baselines = table_ref.shape[1]
    gc = GROUPS * CHANNELS
    rows_of = 2 * gc + 8
    lanes = SUB * TIME
    tiles = baselines // (8 * SUB)
    halves = lanes // 128

    for g in range(GROUPS):
        part = arrived_ref[g * CHANNELS : (g + 1) * CHANNELS]
        gain_ref[g * 8 : g * 8 + 8] = jnp.concatenate([part[:, 0, :], part[:, 1, :]], axis=0)
    pieces = jnp.concatenate(split3(gain_ref[...]), axis=0)
    station = lax.broadcasted_iota(jnp.int32, (stations, baselines), 0)

    def picked(row):
        ids = table_ref[row : row + 1, :]
        one_hot = jnp.where(station == ids, 1.0, 0.0).astype(jnp.bfloat16)
        found = jnp.dot(pieces, one_hot, preferred_element_type=jnp.float32)
        n = 2 * gc
        return found[:n] + found[n : 2 * n] + found[2 * n :]

    first = picked(0)
    second = picked(1)
    def swapped(rows):
        return pltpu.roll(rows.reshape(GROUPS, 8, baselines), 4, 1).reshape(2 * gc, baselines)

    straight = first * second
    crossed = first * swapped(second)
    part = lax.broadcasted_iota(jnp.int32, (2 * gc, baselines), 0) & CHANNELS
    pair = jnp.where(part == 0, straight + swapped(straight), crossed - swapped(crossed))
    starts = table_ref[2:3, :].astype(jnp.float32)
    inverse = table_ref[3:4, :].astype(jnp.float32) * (1.0 / TIME)
    narrow = jnp.concatenate(
        [pair, starts, inverse, jnp.zeros((6, baselines), jnp.float32)], axis=0
    )
    high = narrow.astype(jnp.bfloat16).astype(jnp.float32)
    narrow_ref[0] = high
    narrow_ref[1] = narrow - high
    per_tile = 8 * SUB
    spread = jnp.where(
        lax.broadcasted_iota(jnp.int32, (per_tile, lanes), 0) & (SUB - 1)
        == lax.shift_right_logical(lax.broadcasted_iota(jnp.int32, (per_tile, lanes), 1), 4),
        1.0,
        0.0,
    ).astype(jnp.bfloat16)
    spread = jnp.concatenate([spread, spread], axis=0)
    in_sublane = jnp.where(
        lax.broadcasted_iota(jnp.int32, (8, per_tile), 0)
        == lax.shift_right_logical(lax.broadcasted_iota(jnp.int32, (8, per_tile), 1), 4),
        1.0,
        0.0,
    )
    for q in range(tiles):
        at = slice(q * per_tile, (q + 1) * per_tile)
        for r in range(rows_of):
            for part in range(2):
                staged_ref[r * 8 : r * 8 + 8, part * per_tile : (part + 1) * per_tile] = (
                    narrow_ref[part, r : r + 1, at] * in_sublane
                )
        wide_ref[q] = jnp.dot(
            staged_ref[...].astype(jnp.bfloat16), spread, preferred_element_type=jnp.float32
        )

    for c in range(CHANNELS):
        for j in range(halves * tiles):
            q, lane = j // halves, slice(j % halves * 128, (j % halves + 1) * 128)
            at = slice(j * 128, (j + 1) * 128)
            real = jnp.zeros((8, 128), jnp.float32)
            imag = jnp.zeros((8, 128), jnp.float32)
            for g in range(GROUPS):
                top = (g * 2 * CHANNELS + c) * 8
                gain_real = wide_ref[q, top : top + 8, lane]
                gain_imag = wide_ref[q, top + 8 * CHANNELS : top + 8 * CHANNELS + 8, lane]
                cs = sums_ref[0, g * CHANNELS + c, :, at]
                sn = sums_ref[1, g * CHANNELS + c, :, at]
                real += gain_real * cs + gain_imag * sn
                imag += gain_imag * cs - gain_real * sn
            model_ref[j, c * 16 : c * 16 + 8, :] = real
            model_ref[j, c * 16 + 8 : c * 16 + 16, :] = imag

    slot_ref[...] = jnp.zeros_like(slot_ref)
    start_row = 2 * gc * 8
    inverse_row = start_row + 8
    sample = (lax.broadcasted_iota(jnp.int32, (8, lanes), 1) & (TIME - 1)).astype(jnp.float32)
    targets = [
        wide_ref[q, start_row : start_row + 8, :]
        + jnp.floor(sample * wide_ref[q, inverse_row : inverse_row + 8, :])
        for q in range(tiles)
    ]
    targets.append(jnp.zeros((128 - 8 * tiles, lanes), jnp.float32))
    target_of = jnp.concatenate(targets, axis=0).T
    slot = lax.broadcasted_iota(jnp.int32, (1, WINDOW), 1)
    for sub in range(8 * tiles):
        q, s = sub // 8, sub % 8
        base = pl.multiple_of(base_ref[sub], 128)
        here = (slot + base).astype(jnp.float32)
        chosen = jnp.where(target_of[:, sub : sub + 1] == here, 1.0, 0.0).astype(jnp.bfloat16)
        values = jnp.concatenate(
            [model_ref[q * halves + h, pl.ds(s, 8, stride=8), :] for h in range(halves)], axis=1
        )
        values = values * wide_ref[q, inverse_row + s : inverse_row + s + 1, :]
        high = values.astype(jnp.bfloat16).astype(jnp.float32)
        both = jnp.concatenate([high, values - high], axis=0).astype(jnp.bfloat16)
        placed = jnp.dot(both, chosen, preferred_element_type=jnp.float32)
        slot_ref[:, pl.ds(base, WINDOW)] += placed[:8] + placed[8:]
    capacity = observed_ref.shape[2]
    for c in range(CHANNELS):
        out_ref[c] = observed_ref[c] - slot_ref[2 * c : 2 * c + 2, :capacity]


def on_device(
    observed,
    baseline_uvw_rows,
    frequencies,
    source_offset,
    source_flux,
    source_group,
    direction_gain,
    station_first,
    station_second,
    average_exponent,
    owner_plan,
):
    owners = lax.axis_size("bl")
    me = lax.axis_index("bl")
    my_dir = lax.axis_index("dir")
    local_channels = observed.shape[0]
    capacity = observed.shape[2]
    block_rows = BLOCK_BASELINES * TIME
    f32 = jnp.float32

    send = pl.pallas_call(
        route_kernel,
        out_shape=jax.ShapeDtypeStruct((owners, 3, block_rows), f32),
        in_specs=[SMEM, VMEM],
        out_specs=VMEM,
        name="route",
    )(owner_plan, baseline_uvw_rows)
    arrived = lax.all_to_all(send, "bl", 0, 0, tiled=True)
    gains = lax.all_to_all(direction_gain[0], "dir", 0, 0, tiled=True)

    mine = (owner_plan == me)[:, :, None]
    per_block = (owners, owners, BLOCK_BASELINES)

    def own(ids):
        held = jnp.sum(jnp.where(mine, ids.reshape(per_block), 0), axis=1, dtype=jnp.int32)
        return held

    own_first, own_second, own_exponent = own(station_first), own(station_second), own(average_exponent)
    baselines = own_first.size
    counts = jnp.right_shift(TIME, own_exponent).reshape(-1)
    earlier = jnp.arange(baselines)[:, None] < jnp.arange(baselines)[None, :]
    starts = jnp.sum(jnp.where(earlier, counts[:, None], 0), axis=0, dtype=jnp.int32)
    held = (own_first, own_second, starts.reshape(owners, -1), counts.reshape(owners, -1))
    table = jnp.stack([h.reshape(-1) for h in held])
    base = (table[2].reshape(-1, SUB)[:, 0] // 128) * 128

    number = jnp.arange(source_group.shape[0])
    before = (source_group[:, None] == source_group[None, :]) & (number[:, None] < number[None, :])
    place = source_group * PER_GROUP + jnp.sum(before, axis=0, dtype=jnp.int32)
    order = place[:, None] == number[None, :]
    own_flux = lax.dynamic_slice_in_dim(source_flux, my_dir * local_channels, local_channels, 0)
    values = jnp.concatenate([source_offset, own_flux], axis=0)
    values = jnp.sum(jnp.where(order[None], values[:, :, None], 0.0), axis=1)
    east, north = values[0], values[1]
    depth = jnp.sqrt(1.0 - east * east - north * north) - 1.0
    flux = values[2:]
    total = jnp.sum(flux.reshape(local_channels, GROUPS, PER_GROUP), axis=2)
    own_freq = lax.dynamic_slice_in_dim(frequencies, my_dir * local_channels, local_channels, 0)
    offsets = jnp.stack([east, north, depth]) * own_freq[0]
    ratios = own_freq / own_freq[0]

    gc = GROUPS * local_channels
    tiles = baselines // (8 * SUB)
    lanes = SUB * TIME
    sums = pl.pallas_call(
        sums_kernel,
        out_shape=jax.ShapeDtypeStruct((2, gc, 8, tiles * lanes), f32),
        in_specs=[SMEM] * 4 + [VMEM],
        out_specs=VMEM,
        scratch_shapes=[
            pltpu.VMEM((3, 8, tiles * lanes), f32),
            pltpu.VMEM((PER_GROUP, 8, tiles * lanes), f32),
        ],
        compiler_params=pltpu.CompilerParams(vmem_limit_bytes=24 << 20),
        cost_estimate=pl.CostEstimate(flops=50 * 10**9, bytes_accessed=10**6, transcendentals=0),
        name="sums",
    )(offsets, flux, ratios, total, arrived)
    return pl.pallas_call(
        finish_kernel,
        out_shape=jax.ShapeDtypeStruct(observed.shape, f32),
        in_specs=[SMEM] + [VMEM] * 4,
        out_specs=VMEM,
        scratch_shapes=[
            pltpu.VMEM((tiles, (2 * gc + 8) * 8, lanes), f32),
            pltpu.VMEM((tiles * lanes // 128, 2 * CHANNELS * 8, 128), f32),
            pltpu.VMEM((2 * CHANNELS, capacity + WINDOW), f32),
            pltpu.VMEM((2 * gc, direction_gain.shape[3]), f32),
            pltpu.VMEM((2, 2 * gc + 8, baselines), f32),
            pltpu.VMEM(((2 * gc + 8) * 8, 16 * SUB), f32),
        ],
        compiler_params=pltpu.CompilerParams(vmem_limit_bytes=24 << 20),
        name="finish",
    )(base, table, observed, sums, gains)


def solution(mesh):
    in_specs = (
        P("dir", None, "bl"),
        P(None, "bl"),
        P(),
        P(),
        P(),
        P(),
        P("dir", None, None, None),
        P(),
        P(),
        P(),
        P(),
    )
    return jax.shard_map(
        on_device, mesh=mesh, in_specs=in_specs, out_specs=P("dir", None, "bl"), check_vma=False
    )
```

time: 50 us -> 49.2 us (0.984)
  waiting for transfers between devices: 8.83 us -> 1.09 us
  other arithmetic: 0.97 us -> 3.25 us
  local copies, waits for them, and re-layouts: 1.01 us -> 3.21 us
  starting transfers between devices: 11.7 us -> 13.6 us
  Pallas kernels: 26.9 us -> 27.4 us
    all_to_all x1 -> x2, waiting for transfers between devices: 8.83 us -> 1.09 us  [the longest x1 1.09 us: on_device(): arrived = lax.all_to_all(send, 'bl', 0, 0, tiled=True)]
    reshape x3, local copies, waits for them, and re-layouts: 0.24 us -> 2.51 us  [own(): ids.reshape(per_block)]
    all_to_all x1 -> x2, starting transfers between devices: 11.7 us -> 13.6 us  [the longest x1 8.45 us: on_device(): arrived = lax.all_to_all(send, 'bl', 0, 0, tiled=True)]
    reduce_sum x1, other arithmetic: 0.12 us -> 0.87 us  [on_device(): place = source_group * PER_GROUP + jnp.sum(before, axis=0, dtype=jnp.int32)]
    eq x1, other arithmetic: 0.01 us -> 0.7 us  [on_device(): mine = (owner_plan == me)[:, :, None]]
    add x1, other arithmetic: 0.01 us -> 0.69 us  [on_device(): place = source_group * PER_GROUP + jnp.sum(before, axis=0, dtype=jnp.int32)]
    pallas_call x2 -> x3, Pallas kernels: 26.9 us -> 27.4 us  [the longest x1 21.9 us: on_device(): pl.pallas_call(sums_kernel, out_shape=jax.ShapeDtypeStruct((2, gc, 8, til...]
  transfers between devices with their start and end apart: 1 -> 2, of which waited for: 1 -> 1; matrix products, arithmetic and copies ran while one was open for 4% -> 13% of each run, Pallas kernels for 0% -> 45%
where the time goes in v3:
time: 49.2 us; the launch traced here: 48.7 us
  Pallas kernels  27.4 us (56%)
  starting transfers between devices  13.6 us (28%)
  other arithmetic  3.25 us (7%)
  local copies, waits for them, and re-layouts  3.21 us (7%)
  waiting for transfers between devices  1.09 us (2%)
    pallas_call x1, Pallas kernels, on_device(): pl.pallas_call(sums_kernel, out_shape=jax.ShapeDtypeStruct((2, gc, 8, til...  21.9 us
    all_to_all x1, starting transfers between devices, on_device(): arrived = lax.all_to_all(send, 'bl', 0, 0, tiled=True)  8.45 us
    all_to_all x1, starting transfers between devices, on_device(): gains = lax.all_to_all(direction_gain[0], 'dir', 0, 0, tiled=True)  5.15 us
    pallas_call x1, Pallas kernels, on_device(): pl.pallas_call(finish_kernel, out_shape=jax.ShapeDtypeStruct(observed.sha...  3.86 us
    reshape x3, local copies, waits for them, and re-layouts, own(): ids.reshape(per_block)  2.51 us
    pallas_call x1, Pallas kernels, on_device(): pl.pallas_call(route_kernel, out_shape=jax.ShapeDtypeStruct((owners, 3, b...  1.61 us
    all_to_all x1, waiting for transfers between devices, on_device(): arrived = lax.all_to_all(send, 'bl', 0, 0, tiled=True)  1.09 us
  transfers between devices with their start and end apart: 2, of which 1 were waited for; matrix products, arithmetic and copies ran while one was open for 13% of the time, Pallas kernels for 45%

profile of v3, /device:TPU:1, one launch (start us, length us, event | category | flops | bytes accessed | tf_op | source)
XLA Modules:
  0.0 48.7 jit_solution(1699840845780439876)
XLA Ops:
  0.0 0.0 copy-start
  0.0 1.6 %route.1 = f32[16,3,512]{2,1,0:T(4,128)} custom-call(s32[16,16]{1,0:T(8,128)} %plan_ref.1, f32[3,8192]{1,0:T(4,128)} %uvw_ref.1), custom_call_target="tpu_custom_call" | custom-call | tf_op jit(solution)/shard_map/route/pallas_call | solution.py:240
  1.6 8.4 %all-to-all-start = ((f32[16,3,512]{2,1,0:T(4,128)}), f32[16,3,512]{2,1,0:T(4,128)S(1)}, u32[]{:S(2)}, u32[]{:S(2)}) async-start(f32[16,3,512]{2,1,0:T(4,128)} %route.1), calls=%async_computation | async-start | bytes 262144 | tf_op jit(solution)/shard_map/all_to_all | solution.py:247
  10.1 0.8 %reshape.54 = s32[16,16,32]{2,1,0:T(8,128)S(1)} reshape(s32[8192]{0:T(1024)} %param.18) | data formatting | bytes 65536 | tf_op jit(solution)/shard_map/reshape | solution.py:254
  10.9 0.7 %broadcast_compare_fusion = pred[16,16]{1,0:T(8,128)(4,1)S(1)} fusion(s32[16,16]{1,0:T(8,128)} %plan_ref.1, s32[]{:T(128)S(6)} %axis_index.22), kind=kLoop, calls=%fused_computation.14 | loop fusion | flops 256 | bytes 1284 | tf_op jit(solution)/shard_map/eq | solution.py:250
  11.6 0.8 %reshape.55 = s32[16,16,32]{2,1,0:T(8,128)S(1)} reshape(s32[8192]{0:T(1024)} %param.19) | data formatting | bytes 65536 | tf_op jit(solution)/shard_map/reshape | solution.py:254
  12.5 0.8 %reshape.53 = s32[16,16,32]{2,1,0:T(8,128)S(1)} reshape(s32[8192]{0:T(1024)} %param.20) | data formatting | bytes 65536 | tf_op jit(solution)/shard_map/reshape | solution.py:254
  13.3 0.2 select_reduce_fusion.3
  13.5 0.1 shift_right_arithmetic.25
  13.6 0.1 shift_right_arithmetic.26
  13.7 0.9 %convert_reduce_fusion = s32[256]{0:T(256)S(1)} fusion(s32[256]{0:T(256)} %param.16), kind=kLoop, calls=%fused_computation.4 | loop fusion | flops 327424 | bytes 2048 | tf_op jit(solution)/shard_map/reduce_sum | solution.py:268
  14.5 0.7 %multiply_add_fusion = s32[256]{0:T(256)S(1)} fusion(s32[256]{0:T(256)S(1)} %convert_reduce_fusion, s32[256]{0:T(256)} %param.16), kind=kLoop, calls=%fused_computation.25 | loop fusion | flops 512 | bytes 3072 | tf_op jit(solution)/shard_map/add | solution.py:268
  15.2 0.1 iota_compare_fusion.1
  15.3 0.0 copy-done
  15.3 0.0 copy-done.2
  15.4 0.3 select_reduce_fusion
  15.7 0.1 select_reduce_fusion.1
  15.9 0.1 reshape_squeeze_stack_reshape_reshape.3
  15.9 0.1 slice_reduce_fusion
  16.1 0.1 stack_reshape.7
  16.1 0.1 stack_reshape.6
  16.2 0.1 dynamic_slice.7
  16.3 0.1 reshape.56
  16.4 0.1 reduce_sum.69.total_ref
  16.5 0.1 maximum_multiply_fusion.offset_ref
  16.6 0.1 broadcast_divide_fusion.freq_ref
  16.7 1.1 %all-to-all-done.arrived_ref = f32[16,3,512]{2,1,0:T(4,128)S(1)} async-done(((f32[16,3,512]{2,1,0:T(4,128)}), f32[16,3,512]{2,1,0:T(4,128)S(1)}, u32[]{:S(2)}, u32[]{:S(2)}) %all-to-all-start) | async-done | bytes 98336 | tf_op jit(solution)/shard_map/all_to_all | solution.py:247
  17.7 5.1 %all-to-all-start.1 = ((f32[32,2,512]{2,1,0:T(2,128)}), f32[32,2,512]{2,1,0:T(2,128)S(1)}, u32[]{:S(2)}, u32[]{:S(2)}) async-start(f32[32,2,512]{2,1,0:T(2,128)} %bitcast.2), calls=%async_computation.1 | async-start | bytes 262144 | tf_op jit(solution)/shard_map/all_to_all | solution.py:248
  22.9 21.9 %sums.1.sums_ref = f32[2,32,8,1024]{3,2,1,0:T(8,128)S(1)} custom-call(f32[3,256]{1,0:T(4,128)S(1)} %maximum_multiply_fusion.offset_ref, f32[4,256]{1,0:T(4,128)S(1)} %slice.29.flux_ref, f32[4]{0:T(128)S(1)} %broadcast_divide_fusion.freq_ref, f32[4,8]{1,0:T(4,128)S(1)} %reduce_sum.69.total_ref, f32[16,3,512]{2,1,0:T(4,128)S(1)} %all-to-all-done.arrived_ref), custom_call_target="tpu_custom_call" | custom-call | flops 49999998976 | bytes 1000000 | tf_op jit(solution)/shard_map/sums/pallas_call | solution.py:284
  44.8 0.0 all-to-all-done.1.arrived_ref
  44.8 0.0 copy-done.1
  44.8 3.9 %finish.1 = f32[4,2,3840]{2,1,0:T(2,128)} custom-call(s32[32]{0:T(128)S(1)} %fusion.3.base_ref, s32[4,512]{1,0:T(4,128)S(1)} %pad_add_fusion.table_ref, f32[4,2,3840]{2,1,0:T(2,128)S(1)} %copy-done.1, f32[2,32,8,1024]{3,2,1,0:T(8,128)S(1)} %sums.1.sums_ref, f32[32,2,512]{2,1,0:T(2,128)S(1)} %all-to-all-done.1.arrived_ref), custom_call_target="tpu_custom_call" | custom-call | tf_op jit(solution)/shard_map/finish/pallas_call | solution.py:297
  (12 shorter events, 0.1 us)
Async XLA Ops:
  0.0 15.3 %copy-start = (f32[32,256]{1,0:T(8,128)S(1)}, f32[32,256]{1,0:T(8,128)}, u32[]{:S(2)}) copy-start(f32[32,256]{1,0:T(8,128)} %param.15) | copy-start | bytes 98308
  0.0 15.3 %copy-start.2 = (f32[2,256]{1,0:T(2,128)S(1)}, f32[2,256]{1,0:T(2,128)}, u32[]{:S(2)}) copy-start(f32[2,256]{1,0:T(2,128)} %param.14) | copy-start | bytes 6148
  0.0 16.2 %copy-start.3 = (f32[32]{0:T(128)S(1)}, f32[32]{0:T(128)}, u32[]{:S(2)}) copy-start(f32[32]{0:T(128)} %param.13) | copy-start | bytes 388
  1.6 16.1 %all-to-all-start = ((f32[16,3,512]{2,1,0:T(4,128)}), f32[16,3,512]{2,1,0:T(4,128)S(1)}, u32[]{:S(2)}, u32[]{:S(2)}) async-start(f32[16,3,512]{2,1,0:T(4,128)} %route.1), calls=%async_computation | async-start | bytes 262144 | tf_op jit(solution)/shard_map/all_to_all | solution.py:247
  17.7 27.0 %all-to-all-start.1 = ((f32[32,2,512]{2,1,0:T(2,128)}), f32[32,2,512]{2,1,0:T(2,128)S(1)}, u32[]{:S(2)}, u32[]{:S(2)}) async-start(f32[32,2,512]{2,1,0:T(2,128)} %bitcast.2), calls=%async_computation.1 | async-start | bytes 262144 | tf_op jit(solution)/shard_map/all_to_all | solution.py:248
  22.9 21.9 %copy-start.1 = (f32[4,2,3840]{2,1,0:T(2,128)S(1)}, f32[4,2,3840]{2,1,0:T(2,128)}, u32[]{:S(2)}) copy-start(f32[4,2,3840]{2,1,0:T(2,128)} %observed_ref.1) | copy-start | bytes 368644

commit v4 on v3

--- a/solution.py
+++ b/solution.py
@@ -82,12 +82,13 @@
             sums_ref[1, g * CHANNELS + c] = sin_sum
 
         channel(0, None)
+        channel(1, freq_ref[1])
 
         def other(c, carry):
             channel(c, freq_ref[c])
             return carry
 
-        return lax.fori_loop(1, CHANNELS, other, carry)
+        return lax.fori_loop(2, CHANNELS, other, carry)
 
     lax.fori_loop(0, GROUPS, group, 0)
 

time: 49.2 us -> 49 us (level)
  no operation moved by 1% of the time
where the time goes in v4:
time: 49 us; the launch traced here: 48.4 us
  Pallas kernels  27.1 us (55%)
  starting transfers between devices  13.6 us (28%)
  other arithmetic  3.25 us (7%)
  local copies, waits for them, and re-layouts  3.21 us (7%)
  waiting for transfers between devices  1.09 us (2%)
    pallas_call x1, Pallas kernels, on_device(): pl.pallas_call(sums_kernel, out_shape=jax.ShapeDtypeStruct((2, gc, 8, til...  21.6 us
    all_to_all x1, starting transfers between devices, on_device(): arrived = lax.all_to_all(send, 'bl', 0, 0, tiled=True)  8.45 us
    all_to_all x1, starting transfers between devices, on_device(): gains = lax.all_to_all(direction_gain[0], 'dir', 0, 0, tiled=True)  5.15 us
    pallas_call x1, Pallas kernels, on_device(): pl.pallas_call(finish_kernel, out_shape=jax.ShapeDtypeStruct(observed.sha...  3.85 us
    reshape x3, local copies, waits for them, and re-layouts, own(): ids.reshape(per_block)  2.51 us
    pallas_call x1, Pallas kernels, on_device(): pl.pallas_call(route_kernel, out_shape=jax.ShapeDtypeStruct((owners, 3, b...  1.61 us
    all_to_all x1, waiting for transfers between devices, on_device(): arrived = lax.all_to_all(send, 'bl', 0, 0, tiled=True)  1.09 us
  transfers between devices with their start and end apart: 2, of which 1 were waited for; matrix products, arithmetic and copies ran while one was open for 13% of the time, Pallas kernels for 45%

profile of v4, /device:TPU:1, one launch (start us, length us, event | category | flops | bytes accessed | tf_op | source)
XLA Modules:
  0.0 48.4 jit_solution(707835253175030485)
XLA Ops:
  0.0 0.0 copy-start
  0.0 1.6 %route.1 = f32[16,3,512]{2,1,0:T(4,128)} custom-call(s32[16,16]{1,0:T(8,128)} %plan_ref.1, f32[3,8192]{1,0:T(4,128)} %uvw_ref.1), custom_call_target="tpu_custom_call" | custom-call | tf_op jit(solution)/shard_map/route/pallas_call | solution.py:241
  1.6 8.4 %all-to-all-start = ((f32[16,3,512]{2,1,0:T(4,128)}), f32[16,3,512]{2,1,0:T(4,128)S(1)}, u32[]{:S(2)}, u32[]{:S(2)}) async-start(f32[16,3,512]{2,1,0:T(4,128)} %route.1), calls=%async_computation | async-start | bytes 262144 | tf_op jit(solution)/shard_map/all_to_all | solution.py:248
  10.1 0.8 %reshape.54 = s32[16,16,32]{2,1,0:T(8,128)S(1)} reshape(s32[8192]{0:T(1024)} %param.18) | data formatting | bytes 65536 | tf_op jit(solution)/shard_map/reshape | solution.py:255
  10.9 0.7 %broadcast_compare_fusion = pred[16,16]{1,0:T(8,128)(4,1)S(1)} fusion(s32[16,16]{1,0:T(8,128)} %plan_ref.1, s32[]{:T(128)S(6)} %axis_index.22), kind=kLoop, calls=%fused_computation.14 | loop fusion | flops 256 | bytes 1284 | tf_op jit(solution)/shard_map/eq | solution.py:251
  11.6 0.8 %reshape.55 = s32[16,16,32]{2,1,0:T(8,128)S(1)} reshape(s32[8192]{0:T(1024)} %param.19) | data formatting | bytes 65536 | tf_op jit(solution)/shard_map/reshape | solution.py:255
  12.5 0.8 %reshape.53 = s32[16,16,32]{2,1,0:T(8,128)S(1)} reshape(s32[8192]{0:T(1024)} %param.20) | data formatting | bytes 65536 | tf_op jit(solution)/shard_map/reshape | solution.py:255
  13.3 0.2 select_reduce_fusion.3
  13.5 0.1 shift_right_arithmetic.25
  13.6 0.1 shift_right_arithmetic.26
  13.7 0.9 %convert_reduce_fusion = s32[256]{0:T(256)S(1)} fusion(s32[256]{0:T(256)} %param.16), kind=kLoop, calls=%fused_computation.4 | loop fusion | flops 327424 | bytes 2048 | tf_op jit(solution)/shard_map/reduce_sum | solution.py:269
  14.5 0.7 %multiply_add_fusion = s32[256]{0:T(256)S(1)} fusion(s32[256]{0:T(256)S(1)} %convert_reduce_fusion, s32[256]{0:T(256)} %param.16), kind=kLoop, calls=%fused_computation.25 | loop fusion | flops 512 | bytes 3072 | tf_op jit(solution)/shard_map/add | solution.py:269
  15.2 0.1 iota_compare_fusion.1
  15.3 0.0 copy-done
  15.3 0.0 copy-done.2
  15.4 0.3 select_reduce_fusion
  15.7 0.1 select_reduce_fusion.1
  15.9 0.1 reshape_squeeze_stack_reshape_reshape.3
  15.9 0.1 slice_reduce_fusion
  16.1 0.1 stack_reshape.7
  16.1 0.1 stack_reshape.6
  16.2 0.0 copy-done.3
  16.2 0.1 dynamic_slice.7
  16.3 0.1 reshape.56
  16.4 0.1 reduce_sum.69.total_ref
  16.5 0.1 maximum_multiply_fusion.offset_ref
  16.6 0.1 broadcast_divide_fusion.freq_ref
  16.7 1.1 %all-to-all-done.arrived_ref = f32[16,3,512]{2,1,0:T(4,128)S(1)} async-done(((f32[16,3,512]{2,1,0:T(4,128)}), f32[16,3,512]{2,1,0:T(4,128)S(1)}, u32[]{:S(2)}, u32[]{:S(2)}) %all-to-all-start) | async-done | bytes 98336 | tf_op jit(solution)/shard_map/all_to_all | solution.py:248
  17.7 5.1 %all-to-all-start.1 = ((f32[32,2,512]{2,1,0:T(2,128)}), f32[32,2,512]{2,1,0:T(2,128)S(1)}, u32[]{:S(2)}, u32[]{:S(2)}) async-start(f32[32,2,512]{2,1,0:T(2,128)} %bitcast.2), calls=%async_computation.1 | async-start | bytes 262144 | tf_op jit(solution)/shard_map/all_to_all | solution.py:249
  22.9 21.6 %sums.1.sums_ref = f32[2,32,8,1024]{3,2,1,0:T(8,128)S(1)} custom-call(f32[3,256]{1,0:T(4,128)S(1)} %maximum_multiply_fusion.offset_ref, f32[4,256]{1,0:T(4,128)S(1)} %slice.29.flux_ref, f32[4]{0:T(128)S(1)} %broadcast_divide_fusion.freq_ref, f32[4,8]{1,0:T(4,128)S(1)} %reduce_sum.69.total_ref, f32[16,3,512]{2,1,0:T(4,128)S(1)} %all-to-all-done.arrived_ref), custom_call_target="tpu_custom_call" | custom-call | flops 49999998976 | bytes 1000000 | tf_op jit(solution)/shard_map/sums/pallas_call | solution.py:285
  44.5 0.0 all-to-all-done.1.arrived_ref
  44.5 3.9 %finish.1 = f32[4,2,3840]{2,1,0:T(2,128)} custom-call(s32[32]{0:T(128)S(1)} %fusion.3.base_ref, s32[4,512]{1,0:T(4,128)S(1)} %pad_add_fusion.table_ref, f32[4,2,3840]{2,1,0:T(2,128)S(1)} %copy-done.1, f32[2,32,8,1024]{3,2,1,0:T(8,128)S(1)} %sums.1.sums_ref, f32[32,2,512]{2,1,0:T(2,128)S(1)} %all-to-all-done.1.arrived_ref), custom_call_target="tpu_custom_call" | custom-call | tf_op jit(solution)/shard_map/finish/pallas_call | solution.py:298
  (12 shorter events, 0.1 us)
Async XLA Ops:
  0.0 15.3 %copy-start = (f32[32,256]{1,0:T(8,128)S(1)}, f32[32,256]{1,0:T(8,128)}, u32[]{:S(2)}) copy-start(f32[32,256]{1,0:T(8,128)} %param.15) | copy-start | bytes 98308
  0.0 15.3 %copy-start.2 = (f32[2,256]{1,0:T(2,128)S(1)}, f32[2,256]{1,0:T(2,128)}, u32[]{:S(2)}) copy-start(f32[2,256]{1,0:T(2,128)} %param.14) | copy-start | bytes 6148
  0.0 16.2 %copy-start.3 = (f32[32]{0:T(128)S(1)}, f32[32]{0:T(128)}, u32[]{:S(2)}) copy-start(f32[32]{0:T(128)} %param.13) | copy-start | bytes 388
  1.6 16.1 %all-to-all-start = ((f32[16,3,512]{2,1,0:T(4,128)}), f32[16,3,512]{2,1,0:T(4,128)S(1)}, u32[]{:S(2)}, u32[]{:S(2)}) async-start(f32[16,3,512]{2,1,0:T(4,128)} %route.1), calls=%async_computation | async-start | bytes 262144 | tf_op jit(solution)/shard_map/all_to_all | solution.py:248
  17.7 26.8 %all-to-all-start.1 = ((f32[32,2,512]{2,1,0:T(2,128)}), f32[32,2,512]{2,1,0:T(2,128)S(1)}, u32[]{:S(2)}, u32[]{:S(2)}) async-start(f32[32,2,512]{2,1,0:T(2,128)} %bitcast.2), calls=%async_computation.1 | async-start | bytes 262144 | tf_op jit(solution)/shard_map/all_to_all | solution.py:249
  22.9 21.6 %copy-start.1 = (f32[4,2,3840]{2,1,0:T(2,128)S(1)}, f32[4,2,3840]{2,1,0:T(2,128)}, u32[]{:S(2)}) copy-start(f32[4,2,3840]{2,1,0:T(2,128)} %observed_ref.1) | copy-start | bytes 368644

commit v5 on v4

--- a/solution.py
+++ b/solution.py
@@ -255,7 +255,11 @@
         held = jnp.sum(jnp.where(mine, ids.reshape(per_block), 0), axis=1, dtype=jnp.int32)
         return held
 
-    own_first, own_second, own_exponent = own(station_first), own(station_second), own(average_exponent)
+    stations = direction_gain.shape[3]
+    packed = own((average_exponent * stations + station_first) * stations + station_second)
+    own_second = packed % stations
+    own_first = packed // stations % stations
+    own_exponent = packed // (stations * stations)
     baselines = own_first.size
     counts = jnp.right_shift(TIME, own_exponent).reshape(-1)
     earlier = jnp.arange(baselines)[:, None] < jnp.arange(baselines)[None, :]

time: 49 us -> 48.8 us (level)
  other arithmetic: 3.25 us -> 5.39 us
  local copies, waits for them, and re-layouts: 3.21 us -> 1.26 us
    reshape x3 -> x1, local copies, waits for them, and re-layouts: 2.51 us -> 0.08 us  [own(): ids.reshape(per_block)]
    add x0 -> x1, other arithmetic: none -> 0.8 us  [on_device(): (average_exponent * stations + station_first) * stations + station_second]
    concatenate x1, other arithmetic: 0.01 us -> 0.69 us  [on_device(): values = jnp.concatenate([source_offset, own_flux], axis=0)]
    div x1, other arithmetic: 0.11 us -> 0.77 us  [on_device(): ratios = own_freq / own_freq[0]]
    dynamic_slice x1, local copies, waits for them, and re-layouts: 0.08 us -> 0.73 us  [on_device(): lax.dynamic_slice_in_dim(frequencies, my_dir * local_channels, local_chan...]
  transfers between devices with their start and end apart: 2 -> 2, of which waited for: 1 -> 1; matrix products, arithmetic and copies ran while one was open for 13% -> 14% of each run, Pallas kernels for 45% -> 45%
where the time goes in v5:
time: 48.8 us; the launch traced here: 48.4 us
  Pallas kernels  27.1 us (56%)
  starting transfers between devices  13.6 us (28%)
  other arithmetic  5.39 us (11%)
  local copies, waits for them, and re-layouts  1.26 us (3%)
  waiting for transfers between devices  0.91 us (2%)
    pallas_call x1, Pallas kernels, on_device(): pl.pallas_call(sums_kernel, out_shape=jax.ShapeDtypeStruct((2, gc, 8, til...  21.6 us
    all_to_all x1, starting transfers between devices, on_device(): arrived = lax.all_to_all(send, 'bl', 0, 0, tiled=True)  8.45 us
    all_to_all x1, starting transfers between devices, on_device(): gains = lax.all_to_all(direction_gain[0], 'dir', 0, 0, tiled=True)  5.15 us
    pallas_call x1, Pallas kernels, on_device(): pl.pallas_call(finish_kernel, out_shape=jax.ShapeDtypeStruct(observed.sha...  3.85 us
    pallas_call x1, Pallas kernels, on_device(): pl.pallas_call(route_kernel, out_shape=jax.ShapeDtypeStruct((owners, 3, b...  1.59 us
  transfers between devices with their start and end apart: 2, of which 1 were waited for; matrix products, arithmetic and copies ran while one was open for 14% of the time, Pallas kernels for 45%

profile of v5, /device:TPU:1, one launch (start us, length us, event | category | flops | bytes accessed | tf_op | source)
XLA Modules:
  0.0 48.4 jit_solution(17012335992013749350)
XLA Ops:
  0.0 0.0 copy-start
  0.0 1.6 %route.1 = f32[16,3,512]{2,1,0:T(4,128)} custom-call(s32[16,16]{1,0:T(8,128)} %plan_ref.1, f32[3,8192]{1,0:T(4,128)} %uvw_ref.1), custom_call_target="tpu_custom_call" | custom-call | tf_op jit(solution)/shard_map/route/pallas_call | solution.py:241
  1.6 8.4 %all-to-all-start = ((f32[16,3,512]{2,1,0:T(4,128)}), f32[16,3,512]{2,1,0:T(4,128)S(1)}, u32[]{:S(2)}, u32[]{:S(2)}) async-start(f32[16,3,512]{2,1,0:T(4,128)} %route.1), calls=%async_computation | async-start | bytes 262144 | tf_op jit(solution)/shard_map/all_to_all | solution.py:248
  10.0 0.9 %convert_reduce_fusion = s32[256]{0:T(256)S(1)} fusion(s32[256]{0:T(256)} %param.16), kind=kLoop, calls=%fused_computation.4 | loop fusion | flops 327424 | bytes 2048 | tf_op jit(solution)/shard_map/reduce_sum | solution.py:273
  10.9 0.7 %multiply_add_fusion.1 = s32[256]{0:T(256)S(1)} fusion(s32[256]{0:T(256)S(1)} %convert_reduce_fusion, s32[256]{0:T(256)} %param.16), kind=kLoop, calls=%fused_computation.44 | loop fusion | flops 512 | bytes 3072 | tf_op jit(solution)/shard_map/add | solution.py:273
  11.6 0.1 iota_compare_fusion.1
  11.7 0.0 copy-done
  11.7 0.7 %pad_maximum_fusion = f32[6,256]{1,0:T(8,128)S(1)} fusion(f32[4,256]{1,0:T(4,128)S(1)} %constant_dynamic-slice_fusion, f32[2,256]{1,0:T(2,128)} %param.14), kind=kLoop, calls=%fused_computation.13 | loop fusion | flops 1536 | bytes 12288 | tf_op jit(solution)/shard_map/concatenate | solution.py:276
  12.4 0.3 select_reduce_fusion
  12.8 0.7 %broadcast_compare_fusion = pred[16,16]{1,0:T(8,128)(4,1)S(1)} fusion(s32[16,16]{1,0:T(8,128)} %plan_ref.1, s32[]{:T(128)S(6)} %axis_index.22), kind=kLoop, calls=%fused_computation.19 | loop fusion | flops 256 | bytes 1284 | tf_op jit(solution)/shard_map/eq | solution.py:251
  13.5 0.8 %multiply_add_fusion = s32[8192]{0:T(1024)S(1)} fusion(s32[8192]{0:T(1024)} %param.19, s32[8192]{0:T(1024)} %param.18, s32[8192]{0:T(1024)} %param.20), kind=kLoop, calls=%fused_computation.8 | loop fusion | flops 32768 | bytes 131072 | tf_op jit(solution)/shard_map/add | solution.py:259
  14.3 0.1 reshape.238
  14.4 0.1 select_reduce_fusion.2
  14.5 0.1 reduce_sum.52
  14.6 0.1 reduce_sum.50
  14.6 0.7 %dynamic_slice.7 = f32[4]{0:T(128)S(1)} dynamic-slice(f32[32]{0:T(128)} %param.13, s32[]{:T(128)S(6)} %select_n.82), dynamic_slice_sizes={4} | dynamic-slice | bytes 36 | tf_op jit(solution)/shard_map/dynamic_slice | solution.py:282
  15.4 0.1 reshape.239
  15.5 0.1 select_reduce_fusion.1
  15.7 0.1 reshape_squeeze_stack_reshape_reshape.3
  15.7 0.1 slice_reduce_fusion
  15.9 0.1 reduce_sum.55.total_ref
  16.0 0.1 maximum_multiply_fusion.offset_ref
  16.0 0.8 %broadcast_divide_fusion.freq_ref = f32[4]{0:T(128)S(1)} fusion(f32[]{:T(128)S(1)} %bitcast.7, f32[32]{0:T(128)} %param.13, s32[]{:T(128)S(6)} %select_n.82), kind=kLoop, calls=%fused_computation.47 | loop fusion | flops 4 | bytes 40 | tf_op jit(solution)/shard_map/div | solution.py:284
  16.8 0.9 %all-to-all-done.arrived_ref = f32[16,3,512]{2,1,0:T(4,128)S(1)} async-done(((f32[16,3,512]{2,1,0:T(4,128)}), f32[16,3,512]{2,1,0:T(4,128)S(1)}, u32[]{:S(2)}, u32[]{:S(2)}) %all-to-all-start) | async-done | bytes 98336 | tf_op jit(solution)/shard_map/all_to_all | solution.py:248
  17.7 5.1 %all-to-all-start.1 = ((f32[32,2,512]{2,1,0:T(2,128)}), f32[32,2,512]{2,1,0:T(2,128)S(1)}, u32[]{:S(2)}, u32[]{:S(2)}) async-start(f32[32,2,512]{2,1,0:T(2,128)} %bitcast.4), calls=%async_computation.1 | async-start | bytes 262144 | tf_op jit(solution)/shard_map/all_to_all | solution.py:249
  22.9 0.0 copy-start.1
  22.9 21.6 %sums.1.sums_ref = f32[2,32,8,1024]{3,2,1,0:T(8,128)S(1)} custom-call(f32[3,256]{1,0:T(4,128)S(1)} %maximum_multiply_fusion.offset_ref, f32[4,256]{1,0:T(4,128)S(1)} %slice.29.flux_ref, f32[4]{0:T(128)S(1)} %broadcast_divide_fusion.freq_ref, f32[4,8]{1,0:T(4,128)S(1)} %reduce_sum.55.total_ref, f32[16,3,512]{2,1,0:T(4,128)S(1)} %all-to-all-done.arrived_ref), custom_call_target="tpu_custom_call" | custom-call | flops 49999998976 | bytes 1000000 | tf_op jit(solution)/shard_map/sums/pallas_call | solution.py:289
  44.5 0.0 all-to-all-done.1.arrived_ref
  44.5 0.0 copy-done.1
  44.5 3.9 %finish.1 = f32[4,2,3840]{2,1,0:T(2,128)} custom-call(s32[32]{0:T(128)S(1)} %fusion.8.base_ref, s32[4,512]{1,0:T(4,128)S(1)} %pad_add_fusion.table_ref, f32[4,2,3840]{2,1,0:T(2,128)S(1)} %copy-done.1, f32[2,32,8,1024]{3,2,1,0:T(8,128)S(1)} %sums.1.sums_ref, f32[32,2,512]{2,1,0:T(2,128)S(1)} %all-to-all-done.1.arrived_ref), custom_call_target="tpu_custom_call" | custom-call | tf_op jit(solution)/shard_map/finish/pallas_call | solution.py:302
  (9 shorter events, 0.1 us)
Async XLA Ops:
  0.0 11.7 %copy-start = (f32[32,256]{1,0:T(8,128)S(1)}, f32[32,256]{1,0:T(8,128)}, u32[]{:S(2)}) copy-start(f32[32,256]{1,0:T(8,128)} %param.15) | copy-start | bytes 98308
  1.6 16.1 %all-to-all-start = ((f32[16,3,512]{2,1,0:T(4,128)}), f32[16,3,512]{2,1,0:T(4,128)S(1)}, u32[]{:S(2)}, u32[]{:S(2)}) async-start(f32[16,3,512]{2,1,0:T(4,128)} %route.1), calls=%async_computation | async-start | bytes 262144 | tf_op jit(solution)/shard_map/all_to_all | solution.py:248
  17.7 26.8 %all-to-all-start.1 = ((f32[32,2,512]{2,1,0:T(2,128)}), f32[32,2,512]{2,1,0:T(2,128)S(1)}, u32[]{:S(2)}, u32[]{:S(2)}) async-start(f32[32,2,512]{2,1,0:T(2,128)} %bitcast.4), calls=%async_computation.1 | async-start | bytes 262144 | tf_op jit(solution)/shard_map/all_to_all | solution.py:249
  22.9 21.6 %copy-start.1 = (f32[4,2,3840]{2,1,0:T(2,128)S(1)}, f32[4,2,3840]{2,1,0:T(2,128)}, u32[]{:S(2)}) copy-start(f32[4,2,3840]{2,1,0:T(2,128)} %observed_ref.1) | copy-start | bytes 368644
